TPU v7x, 128 devices: a whole 4x4x4 slice. The times are simulated.
128 devices in a mesh: inst: 16 (over z_lo, x, core), tp: 8 (over y, z_hi).
Axes of the slice: x: 4, y: 4, z: 4 (z_hi: 2, z_lo: 2; z = z_hi * 2 + z_lo), core: 2. Of those that a mesh axis runs over, the one named last changes fastest.
Arguments:
- inputs: bfloat16 [4, 2048, 5120], P(None, 'inst', 'tp'), may hold values from -6 to 6
- norm_gain: bfloat16 [5120], replicated, may hold values from 0.099609375 to 1.8984375
- query_weight: bfloat16 [5120, 4096], P(None, 'tp'), may hold values from -0.078125 to 0.078125
- key_weight: bfloat16 [5120, 1024], P(None, 'tp'), may hold values from -0.078125 to 0.078125
- value_weight: bfloat16 [5120, 1024], P(None, 'tp'), may hold values from -0.078125 to 0.078125
- output_weight: bfloat16 [4096, 5120], P('tp'), may hold values from -0.09375 to 0.09375
- query_gain: bfloat16 [128], replicated, may hold values from 0.5 to 2
- key_gain: bfloat16 [128], replicated, may hold values from 0.5 to 2
- kv_pool: bfloat16 [12288, 16, 2048], P('inst', None, 'tp'), may hold values from -68 to 68, as said below
- block_table: int32 [2048, 6], P('inst'), may hold values from 0 to 767, as said below
- cache_len: int32 [2048], P('inst'), may hold values from 1 to 96, 98304 in all
- move_block: int32 [4096], P('inst'), may hold values from 0 to 767
- move_target: int32 [4096, 1], P('inst'), may hold values from 0 to 15; in each aligned block of 256 rows (0 to 255, 256 to 511, ...) at most 64 rows name the same one
Outputs:
- mixed_out: bfloat16 [4, 2048, 5120], P(None, 'inst', 'tp')
- arrived: bfloat16 [16384, 16, 2048], P('inst', None, 'tp')
Inputs may be any that keep to these rules, and one draw needn't show every extreme that they name: `block_table`: the rows of one instance name every block of its pool of 768 blocks exactly once. `cache_len`: some row holds exactly 96 tokens. `move_block`: a block of the source instance's pool; a block may be listed more than once. `move_target`: in the 256 moves of one instance no destination is named more than 64 times, and in some instance's list one destination is named exactly 64 times; a destination may be the source itself. `kv_pool`: cached keys and values.
All inputs are finite; a program needn't handle non-finite values. No bound on the sum of `cache_len` on one device may be relied on, other than what follows from the above.
Results may differ from a plain program's by a relative error of at most 0.017.
Values may be sent and summed in bfloat16 or wider, within the bound.
No kernel may reach another device: no remote copies, remote signals or barrier semaphores. Data moves between devices by JAX's collectives and lax.ppermute only.
A program may use at most 192 MiB of HBM per device.

v0:
```python
import jax
import jax.numpy as jnp
from jax import lax
from jax.sharding import PartitionSpec as P

HEAD = 128
CAP = 64


EPSILON = 1e-06


def rms_rows(values, gain_f32):
    mean_square = jnp.mean(values * values, axis=-1, keepdims=True)
    return values * lax.rsqrt(mean_square + EPSILON) * gain_f32


def mix_heads(queries, cache_keys, cache_values, new_keys, new_values, lengths, first_step):
    step_count = queries.shape[0]
    fresh_count = new_keys.shape[0]
    places = cache_keys.shape[1]
    score_scale = HEAD ** (-0.5)
    cache_scores = (
        jnp.einsum("srkgh,rpkh->srkgp", queries, cache_keys, preferred_element_type=jnp.float32)
        * score_scale
    )
    fresh_scores = (
        jnp.einsum("srkgh,urkh->srkgu", queries, new_keys, preferred_element_type=jnp.float32)
        * score_scale
    )
    cache_ok = (jnp.arange(places)[None, :] < lengths[:, None])[None, :, None, None, :]
    fresh_ok = (jnp.arange(fresh_count)[None, :] <= first_step + jnp.arange(step_count)[:, None])[
        :, None, None, None, :
    ]
    cache_scores = jnp.where(cache_ok, cache_scores, -jnp.inf)
    fresh_scores = jnp.where(fresh_ok, fresh_scores, -jnp.inf)
    highest_score = jnp.maximum(
        jnp.max(cache_scores, axis=-1, keepdims=True), jnp.max(fresh_scores, axis=-1, keepdims=True)
    )
    cache_exp = jnp.exp(cache_scores - highest_score)
    fresh_exp = jnp.exp(fresh_scores - highest_score)
    denominator = jnp.sum(cache_exp, axis=-1, keepdims=True) + jnp.sum(
        fresh_exp, axis=-1, keepdims=True
    )
    cache_weights = (cache_exp / denominator).astype(jnp.bfloat16)
    fresh_weights = (fresh_exp / denominator).astype(jnp.bfloat16)
    context = jnp.einsum(
        "srkgp,rpkh->srkgh", cache_weights, cache_values, preferred_element_type=jnp.float32
    )
    context = context + jnp.einsum(
        "srkgu,urkh->srkgh", fresh_weights, new_values, preferred_element_type=jnp.float32
    )
    return context.astype(jnp.bfloat16)


def body(
    inputs,
    norm_gain,
    query_weight,
    key_weight,
    value_weight,
    output_weight,
    query_gain,
    key_gain,
    kv_pool,
    block_table,
    cache_len,
    move_block,
    move_target,
):
    step_count, row_count, piece_width = inputs.shape
    heads_local = key_weight.shape[1] // HEAD
    group_size = query_weight.shape[1] // (heads_local * HEAD)
    cached = kv_pool[block_table].reshape(row_count, -1, heads_local, 2, HEAD)
    cache_keys = cached[:, :, :, 0]
    cache_values = cached[:, :, :, 1]
    gain_norm = norm_gain.astype(jnp.float32)
    gain_query = query_gain.astype(jnp.float32)
    gain_key = key_gain.astype(jnp.float32)
    key_list = []
    value_list = []
    step_outputs = []
    for step_index in range(step_count):
        gathered = lax.all_gather(inputs[step_index : step_index + 1], "tp", axis=2, tiled=True)
        project_count_here = gathered.shape[0]
        flattened = gathered.reshape(project_count_here * row_count, -1).astype(jnp.float32)
        normed = rms_rows(flattened, gain_norm).astype(jnp.bfloat16)
        queries = jnp.dot(normed, query_weight, preferred_element_type=jnp.float32).reshape(
            project_count_here, row_count, heads_local, group_size, HEAD
        )
        queries = rms_rows(queries, gain_query).astype(jnp.bfloat16)
        new_keys = jnp.dot(normed, key_weight, preferred_element_type=jnp.float32).reshape(
            project_count_here, row_count, heads_local, HEAD
        )
        new_keys = rms_rows(new_keys, gain_key).astype(jnp.bfloat16)
        new_values = (
            jnp.dot(normed, value_weight, preferred_element_type=jnp.float32)
            .astype(jnp.bfloat16)
            .reshape(project_count_here, row_count, heads_local, HEAD)
        )
        queries, new_keys, new_values = (queries, new_keys, new_values)
        key_list.append(new_keys)
        value_list.append(new_values)
        context = mix_heads(
            queries,
            cache_keys,
            cache_values,
            jnp.concatenate(key_list, axis=0),
            jnp.concatenate(value_list, axis=0),
            cache_len,
            step_index,
        )
        output_count_here = context.shape[0]
        partial_value = jnp.dot(
            context.reshape(output_count_here * row_count, -1),
            output_weight,
            preferred_element_type=jnp.float32,
        )
        step_outputs.append(
            lax.psum_scatter(
                partial_value.reshape(output_count_here, row_count, -1).astype(jnp.bfloat16),
                "tp",
                scatter_dimension=2,
                tiled=True,
            )
        )
    mixed_out = jnp.concatenate(step_outputs, axis=0)
    instance_count = lax.axis_size("inst")
    own_index = lax.axis_index("inst")
    move_count = move_block.shape[0]
    slot_count = instance_count * CAP
    target = move_target[:, 0]
    move_ids = jnp.arange(move_count, dtype=jnp.int32)
    same_target = target[:, None] == target[None, :]
    earlier = move_ids[None, :] < move_ids[:, None]
    order_in = jnp.sum((same_target & earlier).astype(jnp.int32), axis=1)
    addressed = jnp.stack([target, own_index * CAP + order_in], axis=1)
    everyone = lax.all_gather(addressed, "inst", axis=0, tiled=True)
    every_count = everyone.shape[0]
    slot_ids = jnp.arange(slot_count, dtype=jnp.int32)
    match = (everyone[None, :, 0] == own_index) & (everyone[None, :, 1] == slot_ids[:, None])
    slot_filled = jnp.any(match, axis=1)
    slot_mover = jnp.sum(
        jnp.where(match, jnp.arange(every_count, dtype=jnp.int32)[None, :], 0), axis=1
    )
    moving = jnp.take(kv_pool, move_block, axis=0)
    blank_buffer = jnp.zeros((slot_count,) + kv_pool.shape[1:], kv_pool.dtype)
    shard_piece = lax.all_gather(moving, "inst", axis=0, tiled=True)
    count_here = shard_piece.shape[0]
    usable = slot_filled & (slot_mover >= 0) & (slot_mover < count_here)
    picked = jnp.take(shard_piece, jnp.clip(slot_mover, 0, count_here - 1), axis=0)
    updated = jnp.where(usable[:, None, None], picked, blank_buffer)
    return (mixed_out, updated)


def solution(mesh):
    in_specs = (
        P(None, "inst", "tp"),
        P(),
        P(None, "tp"),
        P(None, "tp"),
        P(None, "tp"),
        P("tp", None),
        P(),
        P(),
        P("inst", None, "tp"),
        P("inst", None),
        P("inst"),
        P("inst"),
        P("inst", None),
    )
    out_specs = (P(None, "inst", "tp"), P("inst", None, "tp"))
    return jax.shard_map(body, mesh=mesh, in_specs=in_specs, out_specs=out_specs, check_vma=False)
```

profile of v0, /device:TPU:1, one launch (start us, length us, event | category | flops | bytes accessed | tf_op | source)
XLA Modules:
  0.0 713.5 jit_solution(386921277341497125)
XLA Ops:
  16.8 7.8 %gather_fusion = bf16[768,16,256]{2,1,0:T(8,128)(2,1)} fusion(bf16[768,16,256]{2,1,0:T(8,128)(2,1)} %param.21, s32[1024]{0:T(1024)S(1)} %pad_clamp_fusion.1), kind=kCustom, calls=%fused_computation | custom fusion | bytes 12585984 | tf_op jit(solution)/shard_map/gather | solution.py:74
  24.7 9.8 %reshape.655 = bf16[128,96,1,2,128]{4,3,1,0,2:T(2,128)(2,1)} reshape(bf16[768,16,256]{2,1,0:T(8,128)(2,1)} %gather_fusion) | data formatting | bytes 12582912 | tf_op jit(solution)/shard_map/reshape | solution.py:74
  34.4 15.2 %fusion.109 = (bf16[128,96,1,1,128]{4,3,1,0,2:T(2,128)(2,1)S(1)}, bf16[128,96,1,1,128]{4,3,1,0,2:T(2,128)(2,1)S(1)}) fusion(bf16[128,96,1,2,128]{4,3,1,0,2:T(2,128)(2,1)} %reshape.655), kind=kLoop, calls=%fused_computation.210 | loop fusion | bytes 12582912 | tf_op jit(solution)/shard_map/slice | solution.py:75
  54.4 8.8 %all-gather.6.cloned.1.call-done = bf16[1,128,5120]{2,1,0:T(8,128)(2,1)} async-done(((bf16[1,128,640]{2,1,0:T(8,128)(2,1)}), bf16[1,128,5120]{2,1,0:T(8,128)(2,1)}) %all-gather.6.cloned.1.call-update) | async-done | bytes 1310736 | tf_op jit(solution)/shard_map/all_gather | solution.py:84
  64.9 48.5 %all-gather.12.cloned.1.call-done = bf16[1,128,5120]{2,1,0:T(8,128)(2,1)} async-done(((bf16[1,128,640]{2,1,0:T(8,128)(2,1)}), bf16[1,128,5120]{2,1,0:T(8,128)(2,1)}) %all-gather.12.cloned.1.call-update) | async-done | bytes 1310736 | tf_op jit(solution)/shard_map/all_gather | solution.py:84
  115.1 48.4 %all-gather.10.cloned.1.call-done = bf16[1,128,5120]{2,1,0:T(8,128)(2,1)} async-done(((bf16[1,128,640]{2,1,0:T(8,128)(2,1)}), bf16[1,128,5120]{2,1,0:T(8,128)(2,1)}) %all-gather.10.cloned.1.call-update) | async-done | bytes 1310736 | tf_op jit(solution)/shard_map/all_gather | solution.py:84
  169.5 44.0 %all-gather.8.cloned.1.call-done = bf16[1,128,5120]{2,1,0:T(8,128)(2,1)} async-done(((bf16[1,128,640]{2,1,0:T(8,128)(2,1)}), bf16[1,128,5120]{2,1,0:T(8,128)(2,1)}) %all-gather.8.cloned.1.call-update) | async-done | bytes 1310736 | tf_op jit(solution)/shard_map/all_gather | solution.py:84
  222.1 3.9 fusion.121
  233.8 6.3 copy.105
  243.8 4.1 fusion.117
  258.1 4.1 copy.107
  265.6 4.1 fusion.114
  272.3 3.8 fusion.115
  280.5 4.1 copy.109
  288.0 4.1 fusion.111
  295.8 3.8 fusion.112
  303.9 4.1 copy.111
  316.9 20.9 %all_gather.22 = s32[4096,2]{0,1:T(2,128)S(1)} all-gather(s32[256,2]{0,1:T(2,128)S(1)} %pad_add_fusion), channel_id=1, replica_groups=mesh['inst'=16,'tp'=8] {'inst'}, dimensions={0}, use_global_device_ids=true | all-gather | bytes 34816 | tf_op jit(solution)/shard_map/all_gather | solution.py:138
  341.4 4.8 select_reduce_fusion
  347.5 149.0 %reduce-scatter.15.cloned.1.call-done = bf16[640,128]{1,0:T(8,128)(2,1)} async-done(((bf16[5120,128]{1,0:T(8,128)(2,1)}), bf16[640,128]{1,0:T(8,128)(2,1)}) %reduce-scatter.15.cloned.1.call-update) | async-done | bytes 163856
  497.8 80.2 %reduce-scatter.17.cloned.1.call-done = bf16[640,128]{1,0:T(8,128)(2,1)} async-done(((bf16[5120,128]{1,0:T(8,128)(2,1)}), bf16[640,128]{1,0:T(8,128)(2,1)}) %reduce-scatter.17.cloned.1.call-update) | async-done | bytes 163856
  579.3 75.7 %reduce-scatter.19.cloned.1.call-done = bf16[640,128]{1,0:T(8,128)(2,1)} async-done(((bf16[5120,128]{1,0:T(8,128)(2,1)}), bf16[640,128]{1,0:T(8,128)(2,1)}) %reduce-scatter.19.cloned.1.call-update) | async-done | bytes 163856
  657.2 41.0 %gather_fusion.2 = bf16[1024,16,256]{2,1,0:T(8,128)(2,1)} fusion(bf16[4096,16,256]{2,1,0:T(8,128)(2,1)} %all-gather.14.cloned.1.call-done, s32[1024]{0:T(1024)S(1)} %broadcast_clamp_fusion), kind=kCustom, calls=%fused_computation.2 | custom fusion | bytes 16781312 | tf_op jit(solution)/shard_map/jit(_take)/gather | solution.py:151
  698.2 7.6 %select_select_fusion = bf16[1024,16,256]{2,1,0:T(8,128)(2,1)} fusion(bf16[1024,16,256]{2,1,0:T(8,128)(2,1)} %gather_fusion.2, pred[1024]{0:T(1024)(128)(4,1)S(1)} %get-tuple-element.13, pred[1024]{0:T(1024)(128)(4,1)S(1)} %get-tuple-element.12), kind=kLoop, calls=%fused_computation.7 | loop fusion | flops 8388608 | bytes 16779264 | tf_op jit(solution)/shard_map/jit(_where)/select_n | solution.py:152
  (223 shorter events, 92.7 us)
Async XLA Ops:
  8.0 218.9 %copy-start = (bf16[5120,128]{1,0:T(8,128)(2,1)S(1)}, bf16[5120,128]{1,0:T(8,128)(2,1)}, u32[]{:S(2)}) copy-start(bf16[5120,128]{1,0:T(8,128)(2,1)} %param.17) | copy-start | bytes 3932164
  8.0 55.2 %all-gather.6.cloned.1.call-start = ((), (), s32[]{:S(2)}) async-start(), calls=%async_computation.4 | async-start | bytes 1474560 | tf_op jit(solution)/shard_map/all_gather | solution.py:84
  10.2 103.2 %all-gather.12.cloned.1.call-start = ((), (), s32[]{:S(2)}) async-start(), calls=%async_computation.7 | async-start | bytes 1474560 | tf_op jit(solution)/shard_map/all_gather | solution.py:84
  10.9 152.6 %all-gather.10.cloned.1.call-start = ((), (), s32[]{:S(2)}) async-start(), calls=%async_computation.6 | async-start | bytes 1474560 | tf_op jit(solution)/shard_map/all_gather | solution.py:84
  11.6 201.9 %all-gather.8.cloned.1.call-start = ((), (), s32[]{:S(2)}) async-start(), calls=%async_computation.5 | async-start | bytes 1474560 | tf_op jit(solution)/shard_map/all_gather | solution.py:84
  12.2 334.0 %reduce-scatter.13.cloned.1.call-start = ((), (), s32[]{:S(2)}) async-start(), calls=%async_computation.9 | async-start | bytes 1474560
  14.6 251.0 %copy-start.10 = (f32[5120]{0:T(1024)}, f32[5120]{0:T(1024)S(1)}, u32[]{:S(2)}) copy-start(f32[5120]{0:T(1024)S(1)} %convert_element_type.199) | copy-start | bytes 61444
  15.9 206.2 %copy-start.15 = (f32[128]{0:T(128)}, f32[128]{0:T(128)S(1)}, u32[]{:S(2)}) copy-start(f32[128]{0:T(128)S(1)} %convert_element_type.201) | copy-start | bytes 1540
  113.4 54.5 %copy-start.4 = (bf16[1,128,5120]{2,1,0:T(8,128)(2,1)S(1)}, bf16[1,128,5120]{2,1,0:T(8,128)(2,1)}, u32[]{:S(2)}) copy-start(bf16[1,128,5120]{2,1,0:T(8,128)(2,1)} %all-gather.12.cloned.1.call-done) | copy-start | bytes 3932164
  168.7 48.9 %copy-start.21 = (f32[128]{0:T(128)}, f32[128]{0:T(128)S(1)}, u32[]{:S(2)}) copy-start(f32[128]{0:T(128)S(1)} %add_rsqrt_fusion.7) | copy-start | bytes 1540
  169.5 48.4 %copy-start.9 = (bf16[1,128,5120]{2,1,0:T(8,128)(2,1)S(1)}, bf16[1,128,5120]{2,1,0:T(8,128)(2,1)}, u32[]{:S(2)}) copy-start(bf16[1,128,5120]{2,1,0:T(8,128)(2,1)} %all-gather.6.cloned.1.call-done) | copy-start | bytes 3932164
  215.2 28.6 %copy-start.24 = (f32[128]{0:T(128)}, f32[128]{0:T(128)S(1)}, u32[]{:S(2)}) copy-start(f32[128]{0:T(128)S(1)} %add_rsqrt_fusion.9) | copy-start | bytes 1540
  222.1 9.8 %slice-start = ((s8[5242880]{0:T(1024)(128)(4,1)}), s8[1048576]{0:T(1024)(128)(4,1)S(1)}, s32[]{:S(2)}) async-start(s8[5242880]{0:T(1024)(128)(4,1)} %bitcast.258), calls=%async_computation.13 | async-start | bytes 2097152
  226.9 5.0 slice-start.1
  243.2 6.2 copy-start.16
  243.2 6.2 copy-start.27
  243.2 253.3 %reduce-scatter.15.cloned.1.call-start = ((), (), s32[]{:S(2)}) async-start(), calls=%async_computation.10 | async-start | bytes 1474560
  265.3 312.7 %reduce-scatter.17.cloned.1.call-start = ((), (), s32[]{:S(2)}) async-start(), calls=%async_computation.11 | async-start | bytes 1474560
  272.3 4.5 copy-start.11
  272.3 4.5 copy-start.23
  287.7 6.6 copy-start.17
  287.7 6.6 copy-start.26
  287.7 367.2 %reduce-scatter.19.cloned.1.call-start = ((), (), s32[]{:S(2)}) async-start(), calls=%async_computation.12 | async-start | bytes 1474560
  311.0 346.2 %all-gather.14.cloned.1.call-start = ((), (), s32[]{:S(2)}) async-start(), calls=%async_computation.8 | async-start | bytes 35651584 | tf_op jit(solution)/shard_map/all_gather | solution.py:148
  (21 other events, 56.9 us)
Sparse Core Ops, SparseCore 0:
  11.8 51.4 all-gather.5
  65.5 47.7 all-gather.11
  115.7 47.7 all-gather.9
  165.7 47.7 all-gather.7
  243.3 72.0 reduce-scatter.12
  319.4 177.0 reduce-scatter.14
  500.2 77.7 reduce-scatter.16
  582.2 72.7 reduce-scatter.18
Sparse Core Ops, SparseCore 1:
  316.8 178.1 all-gather.13
where the time goes:
time: 726 us; the launch traced here: 713 us
  waiting for transfers between devices  457 us (63%)
  local copies, waits for them, and re-layouts  128 us (18%)
  matrix products  55.5 us (8%)
  other arithmetic  34.1 us (5%)
  blocking collectives  20.9 us (3%)
  between operations  16.8 us (2%)
    unnamed x13, waiting for transfers between devices  307 us
    all_gather x4, waiting for transfers between devices, body(): lax.all_gather(inputs[step_index:step_index + 1], 'tp', axis=2, tiled=True)  150 us
    unnamed x91, local copies, waits for them, and re-layouts  43.4 us
    gather x1, local copies, waits for them, and re-layouts, body(): jnp.take(shard_piece, jnp.clip(slot_mover, 0, count_here - 1), axis=0)  41 us
    all_gather x1, blocking collectives, body(): everyone = lax.all_gather(addressed, 'inst', axis=0, tiled=True)  20.9 us
    dot_general x4, matrix products, body(): jnp.dot(normed, query_weight, preferred_element_type=jnp.float32)  15.7 us
    slice x1, local copies, waits for them, and re-layouts, body(): cache_keys = cached[:, :, :, 0]  15.2 us
    dot_general x4, matrix products, mix_heads(): jnp.einsum('srkgh,rpkh->srkgp', queries, cache_keys, preferred_element_ty...  15.1 us
  transfers between devices with their start and end apart: 9, of which 7 were waited for; matrix products, arithmetic and copies ran while one was open for 19% of the time, Pallas kernels for 0%

commit v1 on v0

v1 whole, which is shorter than its diff:
```python
import functools

import jax
import jax.numpy as jnp
from jax import lax
from jax.experimental import pallas as pl
from jax.experimental.pallas import tpu as pltpu
from jax.sharding import PartitionSpec as P

HEAD = 128
CAP = 64
PAGE = 16
EPSILON = 1e-06
GROUP = 8
CHUNKS = 2
NEG = -1e30
MIB = 1024 * 1024

GATHERED = ((0, 0), (0, 1), (1, 0), (3, 0), (2, 0), (1, 1), (3, 1), (2, 1))
SCATTERED = ((2, 0), (1, 1), (2, 1), (3, 0), (1, 0), (3, 1), (0, 0), (0, 1))


def places(relative):
    me = lax.axis_index("tp")
    y, z = me // 2, me % 2
    return jnp.stack([((y + dy) % 4) * 2 + (z + dz) % 2 for dy, dz in relative]).astype(jnp.int32)


def tp_move(array, dy, dz):
    pairs = [(y * 2 + z, ((y + dy) % 4) * 2 + (z + dz) % 2) for y in range(4) for z in range(2)]
    return lax.ppermute(array, "tp", pairs)


def inst_move(array, dz, dx, dc):
    pairs = [
        (z * 8 + x * 2 + c, ((z + dz) % 2) * 8 + ((x + dx) % 4) * 2 + (c + dc) % 2)
        for z in range(2)
        for x in range(4)
        for c in range(2)
    ]
    return lax.ppermute(array, "inst", pairs)


def decode_kernel(
    rows, first_row, sources, targets, table, x0, x1, x2, x3, x4, x5, x6, x7, gain, wq, wk, wv, wo, pool,
    lane_row, query_gain, key_gain, plus, minus, local,
    x_v, wq_v, wk_v, wv_v, wo_v, pool_v, qkv, ctx, out_v, sems,
):
    steps = 4
    groups = 4
    width = x0.shape[2]
    count = steps * rows
    xs = (x0, x1, x2, x3, x4, x5, x6, x7)
    w_copies, o_copies = [], []
    for k in range(8):
        span = pl.ds(pl.multiple_of(sources[k] * width, width), width)
        w_copies.append(
            (
                pltpu.make_async_copy(wq.at[span], wq_v.at[k], sems.at[0, k]),
                pltpu.make_async_copy(wk.at[span], wk_v.at[k], sems.at[1, k]),
                pltpu.make_async_copy(wv.at[span], wv_v.at[k], sems.at[2, k]),
            )
        )
        span = pl.ds(pl.multiple_of(targets[k] * width, 128), width)
        o_copies.append(pltpu.make_async_copy(wo.at[:, span], wo_v.at[k], sems.at[3, k]))
    pool_copy = pltpu.make_async_copy(pool, pool_v, sems.at[4, 0])
    x_copies = [
        pltpu.make_async_copy(xs[k].at[:, pl.ds(first_row, rows)], x_v.at[k], sems.at[5, k])
        for k in range(8)
    ]
    for copy in x_copies:
        copy.start()
    for trio in w_copies:
        for copy in trio:
            copy.start()
    pool_copy.start()
    for copy in o_copies:
        copy.start()

    square = jnp.zeros((count, 1), jnp.float32)
    for k in range(8):
        x_copies[k].wait()
        part = x_v[k].reshape(count, width).astype(jnp.float32)
        square = square + jnp.sum(part * part, axis=1, keepdims=True)
    inverse = lax.rsqrt(square * (1.0 / (8 * width)) + EPSILON)
    for k in range(8):
        for copy in w_copies[k]:
            copy.wait()
        normed = x_v[k].reshape(count, width).astype(jnp.float32) * inverse * gain[sources[k]]
        normed = normed.astype(jnp.bfloat16)
        q_part = jnp.dot(normed, wq_v[k], preferred_element_type=jnp.float32)
        k_part = jnp.dot(normed, wk_v[k], preferred_element_type=jnp.float32)
        v_part = jnp.dot(normed, wv_v[k], preferred_element_type=jnp.float32)
        if k == 0:
            qkv[:, 0:512] = q_part
            qkv[:, 512:640] = k_part
            qkv[:, 640:768] = v_part
        else:
            qkv[:, 0:512] += q_part
            qkv[:, 512:640] += k_part
            qkv[:, 640:768] += v_part
    for head in range(5):
        lanes = slice(head * HEAD, (head + 1) * HEAD)
        raw = qkv[:, lanes]
        mean = jnp.mean(raw * raw, axis=1, keepdims=True)
        head_gain = query_gain[...] if head < 4 else key_gain[...]
        qkv[:, lanes] = raw * lax.rsqrt(mean + EPSILON) * head_gain

    pool_copy.wait()
    height = steps * groups * GROUP
    query_row = lax.broadcasted_iota(jnp.int32, (height, 1), 0) % GROUP
    query_step = lax.broadcasted_iota(jnp.int32, (height, 1), 0) // (groups * GROUP)
    fresh_lane = lax.broadcasted_iota(jnp.int32, (1, steps * GROUP), 1)
    fresh_ok = (fresh_lane % GROUP == query_row) & (fresh_lane // GROUP <= query_step)
    scale = HEAD ** (-0.5)
    contract_last = (((1,), (1,)), ((), ()))

    def attend(i, carry):
        first = pl.multiple_of(i * GROUP, GROUP)

        def tiles(lane):
            return [
                qkv[pl.ds(pl.multiple_of(t * rows + first, GROUP), GROUP), lane * HEAD : (lane + 1) * HEAD]
                for t in range(steps)
            ]

        per_group = [tiles(g) for g in range(groups)]
        queries = jnp.concatenate(
            [per_group[g][t] for t in range(steps) for g in range(groups)], axis=0
        ).astype(jnp.bfloat16)
        fresh_k = jnp.concatenate(tiles(4), axis=0).astype(jnp.bfloat16)
        fresh_v = jnp.concatenate(tiles(5), axis=0).astype(jnp.bfloat16)
        blocks = [pool_v[table[i * (GROUP * 6) + j]] for j in range(GROUP * 6)]
        cached_k = jnp.concatenate([b[:, :HEAD] for b in blocks], axis=0)
        cached_v = jnp.concatenate([b[:, HEAD:] for b in blocks], axis=0)
        scores = lax.dot_general(queries, cached_k, contract_last, preferred_element_type=jnp.float32)
        fresh = lax.dot_general(queries, fresh_k, contract_last, preferred_element_type=jnp.float32)
        scores = jnp.where(lane_row[i] == query_row, scores * scale, NEG)
        fresh = jnp.where(fresh_ok, fresh * scale, NEG)
        top = jnp.maximum(
            jnp.max(scores, axis=1, keepdims=True), jnp.max(fresh, axis=1, keepdims=True)
        )
        weights = jnp.exp(scores - top)
        fresh_weights = jnp.exp(fresh - top)
        total = jnp.sum(weights, axis=1, keepdims=True) + jnp.sum(
            fresh_weights, axis=1, keepdims=True
        )
        mixed = jnp.dot(weights.astype(jnp.bfloat16), cached_v, preferred_element_type=jnp.float32)
        mixed += jnp.dot(
            fresh_weights.astype(jnp.bfloat16), fresh_v, preferred_element_type=jnp.float32
        )
        mixed = mixed / total
        for t in range(steps):
            for g in range(groups):
                at = (t * groups + g) * GROUP
                ctx[
                    pl.ds(pl.multiple_of(t * rows + first, GROUP), GROUP),
                    g * HEAD : (g + 1) * HEAD,
                ] = mixed[at : at + GROUP]
        return carry

    lax.fori_loop(0, rows // GROUP, attend, 0, unroll=2)

    context = ctx[...].astype(jnp.bfloat16)
    outs = [plus.at[0], plus.at[1], minus.at[0], minus.at[1]] + [local.at[j] for j in range(4)]
    out_copies = []
    for k in range(8):
        o_copies[k].wait()
        out_v[k] = jnp.dot(context, wo_v[k], preferred_element_type=jnp.float32).astype(jnp.bfloat16)
        out_copies.append(pltpu.make_async_copy(out_v.at[k], outs[k], sems.at[6, k]))
        out_copies[k].start()
    for copy in out_copies:
        copy.wait()


def decode(
    rows, first_row, sources, targets, table, xs, gain, wq, wk, wv, wo, pool, lane_row, query_gain, key_gain
):
    steps, _, width = xs[0].shape
    count = steps * rows
    bf16, f32 = jnp.bfloat16, jnp.float32
    smem = pl.BlockSpec(memory_space=pltpu.SMEM)
    vmem = pl.BlockSpec(memory_space=pltpu.VMEM)
    hbm = pl.BlockSpec(memory_space=pltpu.HBM)
    return pl.pallas_call(
        functools.partial(decode_kernel, rows, first_row),
        out_shape=(
            jax.ShapeDtypeStruct((2, count, width), bf16),
            jax.ShapeDtypeStruct((2, count, width), bf16),
            jax.ShapeDtypeStruct((4, count, width), bf16),
        ),
        in_specs=[smem] * 3 + [hbm] * 8 + [vmem] + [hbm] * 5 + [vmem] * 3,
        out_specs=(hbm, hbm, hbm),
        scratch_shapes=[
            pltpu.VMEM((8, steps, rows, width), bf16),
            pltpu.VMEM((8, width, wq.shape[1]), bf16),
            pltpu.VMEM((8, width, wk.shape[1]), bf16),
            pltpu.VMEM((8, width, wv.shape[1]), bf16),
            pltpu.VMEM((8, wo.shape[0], width), bf16),
            pltpu.VMEM(pool.shape, bf16),
            pltpu.VMEM((count, 768), f32),
            pltpu.VMEM((count, 512), f32),
            pltpu.VMEM((8, count, width), bf16),
            pltpu.SemaphoreType.DMA((7, 8)),
        ],
        compiler_params=pltpu.CompilerParams(vmem_limit_bytes=60 * MIB),
        cost_estimate=pl.CostEstimate(
            flops=2 * count * 5120 * 1280, bytes_accessed=24 * MIB, transcendentals=0
        ),
        name="decode_rows",
    )(sources, targets, table, *xs, gain, wq, wk, wv, wo, pool, lane_row, query_gain, key_gain)


def slots_kernel(table, order, blocks, *refs):
    outs, (blocks_v, sems) = refs[:-7], refs[-2:]
    stages = refs[-7:-2]
    load = pltpu.make_async_copy(blocks, blocks_v, sems.at[0])
    load.start()
    load.wait()
    copies = []
    if len(outs) == 5:

        def pick(m, carry):
            stages[4][m] = blocks_v[order[m]]
            return carry

        lax.fori_loop(0, outs[4].shape[0], pick, 0, unroll=8)
        copies.append(pltpu.make_async_copy(stages[4], outs[4], sems.at[5]))
        copies[0].start()
    for d in (2, 1, 3, 0):

        def one(j, carry):
            at = table[d * 2 * CAP + j]
            block = blocks_v[jnp.maximum(at, 0)]
            stages[d][j] = jnp.where(at >= 0, block, jnp.zeros_like(block))
            return carry

        lax.fori_loop(0, 2 * CAP, one, 0, unroll=8)
        copies.append(pltpu.make_async_copy(stages[d], outs[d], sems.at[1 + d]))
        copies[-1].start()
    for copy in copies:
        copy.wait()


def fill_slots(table, order, blocks, with_compact):
    smem = pl.BlockSpec(memory_space=pltpu.SMEM)
    hbm = pl.BlockSpec(memory_space=pltpu.HBM)
    tail = blocks.shape[1:]
    heights = [2 * CAP] * 4 + [order.shape[0]] * with_compact
    return pl.pallas_call(
        slots_kernel,
        out_shape=tuple(jax.ShapeDtypeStruct((n,) + tail, blocks.dtype) for n in heights),
        in_specs=[smem, smem, hbm],
        out_specs=(hbm,) * len(heights),
        scratch_shapes=[pltpu.VMEM((2 * CAP,) + tail, blocks.dtype)] * 4
        + [
            pltpu.VMEM((order.shape[0],) + tail, blocks.dtype),
            pltpu.VMEM(blocks.shape, blocks.dtype),
            pltpu.SemaphoreType.DMA((6,)),
        ],
        compiler_params=pltpu.CompilerParams(vmem_limit_bytes=60 * MIB),
        cost_estimate=pl.CostEstimate(flops=0, bytes_accessed=16 * MIB, transcendentals=0),
        name="fill_slots",
    )(table, order, blocks)


def slot_table(target, values, own_z, own_x, own_c):
    order = jnp.arange(target.shape[0], dtype=jnp.int32)
    earlier = (target[:, None] == target[None, :]) & (order[None, :] < order[:, None])
    rank = jnp.sum(earlier.astype(jnp.int32), axis=1)
    slot = jnp.arange(8 * CAP, dtype=jnp.int32)
    far, other = slot // (2 * CAP), (slot // CAP) % 2
    wanted = own_z * 8 + ((own_x + far) % 4) * 2 + (own_c + other) % 2
    match = (wanted * CAP + slot % CAP)[:, None] == (target * CAP + rank)[None, :]
    return jnp.max(jnp.where(match, values[None, :], -1), axis=1)


def cross(received):
    return received + [inst_move(r, 0, 0, 1) for r in received]


def place_kernel(places_ref, *refs):
    pieces, out, stage, sems = refs[:8], refs[-3], refs[-2], refs[-1]
    ins, outs = [], []
    for j in range(8):
        start = pl.multiple_of(places_ref[j] * CAP, CAP)
        part = pieces[j].at[pl.ds((j // 4) * CAP, CAP)]
        ins.append(pltpu.make_async_copy(part, stage.at[j], sems.at[0, j]))
        outs.append(pltpu.make_async_copy(stage.at[j], out.at[pl.ds(start, CAP)], sems.at[1, j]))
    for copy in ins:
        copy.start()
    for j in range(8):
        ins[j].wait()
        outs[j].start()
    for copy in outs:
        copy.wait()


def place_pieces(where, pieces, before):
    smem = pl.BlockSpec(memory_space=pltpu.SMEM)
    either = pl.BlockSpec(memory_space=pl.ANY)
    hbm = pl.BlockSpec(memory_space=pltpu.HBM)
    blocks = pieces[0].shape[1:]
    shape = jax.ShapeDtypeStruct((16 * CAP,) + blocks, pieces[0].dtype)
    extra = [] if before is None else [before]
    return pl.pallas_call(
        place_kernel,
        out_shape=shape,
        in_specs=[smem] + [either] * 8 + [hbm] * len(extra),
        out_specs=hbm,
        scratch_shapes=[
            pltpu.VMEM((8, CAP) + blocks, pieces[0].dtype),
            pltpu.SemaphoreType.DMA((2, 8)),
        ],
        input_output_aliases={} if before is None else {9: 0},
        compiler_params=pltpu.CompilerParams(vmem_limit_bytes=60 * MIB),
        cost_estimate=pl.CostEstimate(flops=0, bytes_accessed=16 * MIB, transcendentals=0),
        name="place_pieces",
    )(where, *pieces, *extra)


def after(array, *others):
    return lax.optimization_barrier((array,) + others)[0]


def gather_rows(x):
    other = tp_move(x, 0, 1)
    up, down = tp_move(x, 3, 0), tp_move(x, 1, 0)
    other_up, other_down = tp_move(other, 3, 0), tp_move(other, 1, 0)
    far = tp_move(down, 1, 0)
    other_far = tp_move(other_up, 3, 0)
    return [x, other, up, down, far, other_up, other_down, other_far]


def scatter_sum(plus, minus, local):
    f32, bf16 = jnp.float32, jnp.bfloat16
    below = tp_move(plus, 1, 0)
    above = tp_move(minus, 3, 0)
    up = (local[0].astype(f32) + below[0].astype(f32)).astype(bf16)
    down = (local[1].astype(f32) + above[0].astype(f32)).astype(bf16)
    from_below = tp_move(up, 1, 0)
    from_above = tp_move(down, 3, 0)
    other = (local[3].astype(f32) + below[1].astype(f32) + from_above.astype(f32)).astype(bf16)
    crossed = tp_move(other, 0, 1)
    mine = local[2].astype(f32) + above[1].astype(f32) + from_below.astype(f32)
    return (mine + crossed.astype(f32)).astype(bf16)


def body(
    inputs,
    norm_gain,
    query_weight,
    key_weight,
    value_weight,
    output_weight,
    query_gain,
    key_gain,
    kv_pool,
    block_table,
    cache_len,
    move_block,
    move_target,
):
    step_count, row_count, width = inputs.shape
    f32 = jnp.float32
    own = lax.axis_index("inst")
    own_z, own_x, own_c = own // 8, (own // 2) % 4, own % 2

    target = move_target[:, 0]
    other_target = inst_move(target, 1, 0, 0)

    rows = row_count // CHUNKS
    gathered = gather_rows(inputs)

    table = slot_table(target, move_block, own_z, own_x, own_c)
    table = after(table, gathered[1])
    *slots, compact = fill_slots(table, move_block, kv_pool, True)
    compact = after(compact, other_target)
    other_target = after(other_target, compact)
    other_blocks = inst_move(compact, 1, 0, 0)
    far = inst_move(slots[2], 0, 2, 0)
    near = inst_move(after(slots[1], far, gathered[5]), 0, 1, 0)
    back = inst_move(after(slots[3], far, gathered[5]), 0, 3, 0)
    order = jnp.arange(move_block.shape[0], dtype=jnp.int32)
    other_table = slot_table(other_target, order, own_z, own_x, own_c)

    gain = norm_gain.astype(f32).reshape(8, 1, width)
    positions = jnp.arange(block_table.shape[1] * PAGE, dtype=jnp.int32)
    lane_row = jnp.where(
        positions[None, :] < cache_len[:, None],
        (jnp.arange(row_count, dtype=jnp.int32) % GROUP)[:, None],
        -1,
    ).reshape(row_count // GROUP, 1, -1)
    sources, targets = places(GATHERED), places(SCATTERED)
    query_gain = query_gain.astype(f32).reshape(1, HEAD)
    key_gain = key_gain.astype(f32).reshape(1, HEAD)
    def where(z):
        return jnp.stack(
            [z * 8 + ((own_x - j % 4) % 4) * 2 + (own_c + j // 4) % 2 for j in range(8)]
        ).astype(jnp.int32)

    arrived = place_pieces(where(own_z), cross([slots[0], near, far, back]), None)

    chunks = []
    for c in range(CHUNKS):
        first = c * rows
        tables = block_table[first : first + rows].reshape(-1)
        lanes = lane_row[first // GROUP : (first + rows) // GROUP]
        if c == 1:
            other_table = after(other_table, parts[0])
            other_slots = fill_slots(other_table, order, other_blocks, False)
            other_near = inst_move(other_slots[1], 0, 1, 0)
            other_back = inst_move(other_slots[3], 0, 3, 0)
            gathered[0] = after(gathered[0], other_slots[0])
        parts = decode(
            rows, first, sources, targets, tables, gathered, gain, query_weight, key_weight,
            value_weight, output_weight, kv_pool, lanes, query_gain, key_gain,
        )
        chunks.append(scatter_sum(*parts).reshape(step_count, rows, width))
    mixed_out = jnp.concatenate(chunks, axis=1)

    other_far = inst_move(after(other_slots[2], arrived, other_near, other_back), 0, 2, 0)
    other_pieces = cross([other_slots[0], other_near, other_far, other_back])
    arrived = place_pieces(where(1 - own_z), other_pieces, arrived)
    return (mixed_out, arrived)


def solution(mesh):
    in_specs = (
        P(None, "inst", "tp"),
        P(),
        P(None, "tp"),
        P(None, "tp"),
        P(None, "tp"),
        P("tp", None),
        P(),
        P(),
        P("inst", None, "tp"),
        P("inst", None),
        P("inst"),
        P("inst"),
        P("inst", None),
    )
    out_specs = (P(None, "inst", "tp"), P("inst", None, "tp"))
    return jax.shard_map(body, mesh=mesh, in_specs=in_specs, out_specs=out_specs, check_vma=False)
```

time: 726 us -> 186 us (0.26); the launches traced: 713 us -> 185 us
  waiting for transfers between devices: 457 us -> 63.1 us
  local copies, waits for them, and re-layouts: 128 us -> 7.95 us
  matrix products: 55.5 us -> 0 us
  Pallas kernels: 0 us -> 50.8 us
  starting transfers between devices: 1.27 us -> 47.6 us
  blocking collectives: 20.9 us -> 0 us
  other arithmetic: 34.1 us -> 14.4 us
  between operations: 16.8 us -> 1.08 us
    unnamed x13 -> x0, waiting for transfers between devices: 307 us -> none
    all_gather x5 -> x0, waiting for transfers between devices: 150 us -> none  [the longest x4 150 us: body(): lax.all_gather(inputs[step_index:step_index + 1], 'tp', axis=2, tiled=True)]
    ppermute x0 -> x33, waiting for transfers between devices: none -> 63.1 us  [the longest x17 43.9 us: tp_move(): return lax.ppermute(array, 'tp', pairs)]
    dot_general x30 -> x0, matrix products: 55.5 us -> none  [the longest x4 15.7 us: body(): jnp.dot(normed, query_weight, preferred_element_type=jnp.float32)]
    gather x3 -> x0, local copies, waits for them, and re-layouts: 52.4 us -> none  [the longest x1 41 us: body(): jnp.take(shard_piece, jnp.clip(slot_mover, 0, count_here - 1), axis=0)]
    pallas_call x0 -> x6, Pallas kernels: none -> 50.8 us  [the longest x2 30.4 us: decode(): pl.pallas_call(functools.partial(decode_kernel, rows, first_row), out_sha...]
    ppermute x0 -> x33, starting transfers between devices: none -> 47.6 us  [the longest x16 24.8 us: inst_move(): return lax.ppermute(array, 'inst', pairs)]
    unnamed x91 -> x46, local copies, waits for them, and re-layouts: 43.4 us -> 1.73 us
  transfers between devices with their start and end apart: 9 -> 33, of which waited for: 7 -> 9; matrix products, arithmetic and copies ran while one was open for 19% -> 11% of each run, Pallas kernels for 0% -> 25%
where the time goes in v1:
time: 186 us; the launch traced here: 185 us
  waiting for transfers between devices  63.1 us (34%)
  Pallas kernels  50.8 us (27%)
  starting transfers between devices  47.6 us (26%)
  other arithmetic  14.4 us (8%)
  local copies, waits for them, and re-layouts  7.95 us (4%)
    ppermute x17, waiting for transfers between devices, tp_move(): return lax.ppermute(array, 'tp', pairs)  43.9 us
    pallas_call x2, Pallas kernels, decode(): pl.pallas_call(functools.partial(decode_kernel, rows, first_row), out_sha...  30.4 us
    ppermute x16, starting transfers between devices, inst_move(): return lax.ppermute(array, 'inst', pairs)  24.8 us
    ppermute x17, starting transfers between devices, tp_move(): return lax.ppermute(array, 'tp', pairs)  22.8 us
    ppermute x16, waiting for transfers between devices, inst_move(): return lax.ppermute(array, 'inst', pairs)  19.2 us
    pallas_call x2, Pallas kernels, fill_slots(): pl.pallas_call(slots_kernel, out_shape=tuple((jax.ShapeDtypeStruct((n,) +...  11.7 us
    pallas_call x2, Pallas kernels, place_pieces(): pl.pallas_call(place_kernel, out_shape=shape, in_specs=[smem] + [either]...  8.62 us
  transfers between devices with their start and end apart: 33, of which 9 were waited for; matrix products, arithmetic and copies ran while one was open for 11% of the time, Pallas kernels for 25%

profile of v1, /device:TPU:1, one launch (start us, length us, event | category | flops | bytes accessed | tf_op | source)
XLA Modules:
  0.0 184.9 jit_solution(16350221992648368130)
XLA Ops:
  0.6 4.5 %collective-permute-start = (bf16[4,128,640]{2,1,0:T(8,128)(2,1)}, bf16[4,128,640]{2,1,0:T(8,128)(2,1)S(1)}, u32[]{:S(2)}, u32[]{:S(2)}) collective-permute-start(bf16[4,128,640]{2,1,0:T(8,128)(2,1)} %x0.2), channel_id=1, source_target_pairs={{0,1},{1,0},{2,3},{3,2},{4,5},{5,4},{6,7},{7,6},{8,9},{9,8},{10,11... | collective-permute-start | bytes 1966088 | tf_op jit(solution)/shard_map/ppermute | solution.py:31
  8.1 11.7 %collective-permute-done.x1 = bf16[4,128,640]{2,1,0:T(8,128)(2,1)S(1)} collective-permute-done((bf16[4,128,640]{2,1,0:T(8,128)(2,1)}, bf16[4,128,640]{2,1,0:T(8,128)(2,1)S(1)}, u32[]{:S(2)}, u32[]{:S(2)}) %collective-permute-start) | collective-permute-done | bytes 655392 | tf_op jit(solution)/shard_map/ppermute | solution.py:31
  19.8 2.7 %collective-permute-start.4 = (bf16[4,128,640]{2,1,0:T(8,128)(2,1)S(1)}, bf16[4,128,640]{2,1,0:T(8,128)(2,1)S(1)}, u32[]{:S(2)}, u32[]{:S(2)}) collective-permute-start(bf16[4,128,640]{2,1,0:T(8,128)(2,1)S(1)} %collective-permute-done.x1), channel_id=1, source_target_pairs={{0,6},{1,7},{2,0},{3,1},{4,2},{5,3},{6,4},{7,5},{8,14},{9,15},{10,... | collective-permute-start | bytes 1966088 | tf_op jit(solution)/shard_map/ppermute | solution.py:31
  24.1 6.8 %fill_slots.2 = (bf16[128,16,256]{2,1,0:T(8,128)(2,1)}, bf16[128,16,256]{2,1,0:T(8,128)(2,1)}, bf16[128,16,256]{2,1,0:T(8,128)(2,1)}, bf16[128,16,256]{2,1,0:T(8,128)(2,1)}, bf16[256,16,256]{2,1,0:T(8,128)(2,1)}) custom-call(s32[512]{0:T(512)} %select_reduce_fusion.1.table, s32[256]{0:T(256)} %order.1, bf16[768,16,256]{2,1,0:T(8,128)(2,1)} %pool.3), custom_call_target="tpu_custom_call" | custom-call | bytes 16777216 | tf_op jit(solution)/shard_map/fill_slots/pallas_call | solution.py:250
  30.9 2.8 %collective-permute-start.20 = (bf16[128,16,256]{2,1,0:T(8,128)(2,1)}, bf16[128,16,256]{2,1,0:T(8,128)(2,1)S(1)}, u32[]{:S(2)}, u32[]{:S(2)}) collective-permute-start(bf16[128,16,256]{2,1,0:T(8,128)(2,1)} %get-tuple-element.42), channel_id=1, source_target_pairs={{0,32},{8,40},{16,48},{24,56},{32,0},{40,8},{48,16},{56,24},{64,96... | collective-permute-start | bytes 3145736 | tf_op jit(solution)/shard_map/ppermute | solution.py:41
  38.7 17.1 %collective-permute-done.20.refs_2_ = bf16[128,16,256]{2,1,0:T(8,128)(2,1)S(1)} collective-permute-done((bf16[128,16,256]{2,1,0:T(8,128)(2,1)}, bf16[128,16,256]{2,1,0:T(8,128)(2,1)S(1)}, u32[]{:S(2)}, u32[]{:S(2)}) %collective-permute-start.20) | collective-permute-done | bytes 1048608 | tf_op jit(solution)/shard_map/ppermute | solution.py:41
  55.8 2.4 %collective-permute-start.23 = (bf16[128,16,256]{2,1,0:T(8,128)(2,1)}, bf16[128,16,256]{2,1,0:T(8,128)(2,1)}, u32[]{:S(2)}, u32[]{:S(2)}) collective-permute-start(bf16[128,16,256]{2,1,0:T(8,128)(2,1)} %get-tuple-element.40.refs_0_), channel_id=1, source_target_pairs={{0,8},{8,0},{16,24},{24,16},{32,40},{40,32},{48,56},{56,48},{64,72... | collective-permute-start | bytes 3145736 | tf_op jit(solution)/shard_map/ppermute | solution.py:41
  60.1 5.5 %collective-permute-done.5.x6 = bf16[4,128,640]{2,1,0:T(8,128)(2,1)S(1)} collective-permute-done((bf16[4,128,640]{2,1,0:T(8,128)(2,1)S(1)}, bf16[4,128,640]{2,1,0:T(8,128)(2,1)S(1)}, u32[]{:S(2)}, u32[]{:S(2)}) %collective-permute-start.5) | collective-permute-done | bytes 655392 | tf_op jit(solution)/shard_map/ppermute | solution.py:31
  70.5 4.4 %collective-permute-done.6.x7 = bf16[4,128,640]{2,1,0:T(8,128)(2,1)S(1)} collective-permute-done((bf16[4,128,640]{2,1,0:T(8,128)(2,1)S(1)}, bf16[4,128,640]{2,1,0:T(8,128)(2,1)S(1)}, u32[]{:S(2)}, u32[]{:S(2)}) %collective-permute-start.6) | collective-permute-done | bytes 655392 | tf_op jit(solution)/shard_map/ppermute | solution.py:31
  75.7 15.2 %decode_rows.2 = (bf16[2,256,640]{2,1,0:T(8,128)(2,1)}, bf16[2,256,640]{2,1,0:T(8,128)(2,1)}, bf16[4,256,640]{2,1,0:T(8,128)(2,1)}) custom-call(s32[8]{0:T(128)} %stack.100.sources, s32[8]{0:T(128)} %stack.101.targets, s32[384]{0:T(512)} %reshape.153.table, bf16[4,128,640]{2,1,0:T(8,128)(2,1)} %x0.2, bf16[4,128,640]{2,1,0:T(8,128)(2,1)} %copy-done.1, ...), custom_call_target="tpu_custom_call" | custom-call | flops 3355443200 | bytes 25165824 | tf_op jit(solution)/shard_map/decode_rows/pallas_call | solution.py:185
  96.0 5.0 %fill_slots.3 = (bf16[128,16,256]{2,1,0:T(8,128)(2,1)}, bf16[128,16,256]{2,1,0:T(8,128)(2,1)}, bf16[128,16,256]{2,1,0:T(8,128)(2,1)}, bf16[128,16,256]{2,1,0:T(8,128)(2,1)}) custom-call(s32[512]{0:T(512)} %select_reduce_fusion.table, s32[256]{0:T(256)} %iota.34.order, bf16[256,16,256]{2,1,0:T(8,128)(2,1)} %collective-permute-done.13.blocks), custom_call_target="tpu_custom_call" | custom-call | bytes 16777216 | tf_op jit(solution)/shard_map/fill_slots/pallas_call | solution.py:250
  100.9 6.0 %collective-permute-done.7 = bf16[2,256,640]{2,1,0:T(8,128)(2,1)} collective-permute-done((bf16[2,256,640]{2,1,0:T(8,128)(2,1)}, bf16[2,256,640]{2,1,0:T(8,128)(2,1)}, u32[]{:S(2)}, u32[]{:S(2)}) %collective-permute-start.7) | collective-permute-done | bytes 655392 | tf_op jit(solution)/shard_map/ppermute | solution.py:31
  109.6 2.4 %collective-permute-start.27 = (bf16[128,16,256]{2,1,0:T(8,128)(2,1)}, bf16[128,16,256]{2,1,0:T(8,128)(2,1)}, u32[]{:S(2)}, u32[]{:S(2)}) collective-permute-start(bf16[128,16,256]{2,1,0:T(8,128)(2,1)} %get-tuple-element.46), channel_id=1, source_target_pairs={{0,48},{8,56},{16,0},{24,8},{32,16},{40,24},{48,32},{56,40},{64,11... | collective-permute-start | bytes 3145736 | tf_op jit(solution)/shard_map/ppermute | solution.py:41
  113.5 15.2 %decode_rows.3 = (bf16[2,256,640]{2,1,0:T(8,128)(2,1)}, bf16[2,256,640]{2,1,0:T(8,128)(2,1)}, bf16[4,256,640]{2,1,0:T(8,128)(2,1)}) custom-call(s32[8]{0:T(128)} %stack.100.sources, s32[8]{0:T(128)} %stack.101.targets, s32[384]{0:T(512)} %reshape.161.table, bf16[4,128,640]{2,1,0:T(8,128)(2,1)} %x0.2, bf16[4,128,640]{2,1,0:T(8,128)(2,1)} %copy-done.1, ...), custom_call_target="tpu_custom_call" | custom-call | flops 3355443200 | bytes 25165824 | tf_op jit(solution)/shard_map/decode_rows/pallas_call | solution.py:185
  130.3 2.1 %fusion.6 = (bf16[256,640]{1,0:T(8,128)(2,1)}, bf16[256,640]{1,0:T(8,128)(2,1)}) fusion(bf16[2,256,640]{2,1,0:T(8,128)(2,1)} %collective-permute-done.8, bf16[4,256,640]{2,1,0:T(8,128)(2,1)S(1)} %copy-done.8, bf16[2,256,640]{2,1,0:T(8,128)(2,1)} %collective-permute-done.7), kind=kLoop, calls=%fused_computation.17 | loop fusion | flops 1310720 | bytes 1966080 | tf_op jit(solution)/shard_map/convert_element_type | solution.py:339
  134.9 4.4 %place_pieces.2.refs_8_ = bf16[1024,16,256]{2,1,0:T(8,128)(2,1)} custom-call(s32[8]{0:T(128)} %stack.119.places_ref, bf16[128,16,256]{2,1,0:T(8,128)(2,1)} %get-tuple-element.40.refs_0_, bf16[128,16,256]{2,1,0:T(8,128)(2,1)} %collective-permute-done.21.refs_1_, bf16[128,16,256]{2,1,0:T(8,128)(2,1)} %copy-done.10, ...), custom_call_target="tpu_custom_call" | custom-call | bytes 16777216 | tf_op jit(solution)/shard_map/place_pieces/pallas_call | solution.py:306
  140.7 9.6 %collective-permute-done.10 = bf16[256,640]{1,0:T(8,128)(2,1)} collective-permute-done((bf16[256,640]{1,0:T(8,128)(2,1)}, bf16[256,640]{1,0:T(8,128)(2,1)}, u32[]{:S(2)}, u32[]{:S(2)}) %collective-permute-start.10) | collective-permute-done | bytes 327712 | tf_op jit(solution)/shard_map/ppermute | solution.py:31
  151.5 2.7 %collective-permute-start.11 = (bf16[256,640]{1,0:T(8,128)(2,1)S(1)}, bf16[256,640]{1,0:T(8,128)(2,1)S(1)}, u32[]{:S(2)}, u32[]{:S(2)}) collective-permute-start(bf16[256,640]{1,0:T(8,128)(2,1)S(1)} %fusion.3), channel_id=1, source_target_pairs={{0,1},{1,0},{2,3},{3,2},{4,5},{5,4},{6,7},{7,6},{8,9},{9,8},{10,11... | collective-permute-start | bytes 983048 | tf_op jit(solution)/shard_map/ppermute | solution.py:31
  157.2 3.6 %collective-permute-start.29 = (bf16[128,16,256]{2,1,0:T(8,128)(2,1)}, bf16[128,16,256]{2,1,0:T(8,128)(2,1)}, u32[]{:S(2)}, u32[]{:S(2)}) collective-permute-start(bf16[128,16,256]{2,1,0:T(8,128)(2,1)} %get-tuple-element.33.refs_0_), channel_id=1, source_target_pairs={{0,8},{8,0},{16,24},{24,16},{32,40},{40,32},{48,56},{56,48},{64,72... | collective-permute-start | bytes 3145736 | tf_op jit(solution)/shard_map/ppermute | solution.py:41
  160.9 2.3 %collective-permute-start.30 = (bf16[128,16,256]{2,1,0:T(8,128)(2,1)}, bf16[128,16,256]{2,1,0:T(8,128)(2,1)}, u32[]{:S(2)}, u32[]{:S(2)}) collective-permute-start(bf16[128,16,256]{2,1,0:T(8,128)(2,1)} %collective-permute-done.19.refs_1_), channel_id=1, source_target_pairs={{0,8},{8,0},{16,24},{24,16},{32,40},{40,32},{48,56},{56,48},{64,72... | collective-permute-start | bytes 3145736 | tf_op jit(solution)/shard_map/ppermute | solution.py:41
  163.2 2.7 %collective-permute-start.32 = (bf16[128,16,256]{2,1,0:T(8,128)(2,1)}, bf16[128,16,256]{2,1,0:T(8,128)(2,1)}, u32[]{:S(2)}, u32[]{:S(2)}) collective-permute-start(bf16[128,16,256]{2,1,0:T(8,128)(2,1)} %collective-permute-done.27.refs_3_), channel_id=1, source_target_pairs={{0,8},{8,0},{16,24},{24,16},{32,40},{40,32},{48,56},{56,48},{64,72... | collective-permute-start | bytes 3145736 | tf_op jit(solution)/shard_map/ppermute | solution.py:41
  168.6 2.6 %collective-permute-start.18 = (bf16[256,640]{1,0:T(8,128)(2,1)S(1)}, bf16[256,640]{1,0:T(8,128)(2,1)}, u32[]{:S(2)}, u32[]{:S(2)}) collective-permute-start(bf16[256,640]{1,0:T(8,128)(2,1)S(1)} %fusion), channel_id=1, source_target_pairs={{0,1},{1,0},{2,3},{3,2},{4,5},{5,4},{6,7},{7,6},{8,9},{9,8},{10,11... | collective-permute-start | bytes 983048 | tf_op jit(solution)/shard_map/ppermute | solution.py:31
  173.1 5.2 %collective-permute-done.18 = bf16[256,640]{1,0:T(8,128)(2,1)} collective-permute-done((bf16[256,640]{1,0:T(8,128)(2,1)S(1)}, bf16[256,640]{1,0:T(8,128)(2,1)}, u32[]{:S(2)}, u32[]{:S(2)}) %collective-permute-start.18) | collective-permute-done | bytes 327712 | tf_op jit(solution)/shard_map/ppermute | solution.py:31
  180.5 4.2 %place_pieces.3 = bf16[1024,16,256]{2,1,0:T(8,128)(2,1)} custom-call(s32[8]{0:T(128)} %stack.110.places_ref, bf16[128,16,256]{2,1,0:T(8,128)(2,1)} %get-tuple-element.33.refs_0_, bf16[128,16,256]{2,1,0:T(8,128)(2,1)} %collective-permute-done.19.refs_1_, bf16[128,16,256]{2,1,0:T(8,128)(2,1)} %collective-permute-done.28.refs_2_, ...), custom_call_target="tpu_custom_call", output_to_operand_aliasing={{}: (9, {})} | custom-call | bytes 16777216 | tf_op jit(solution)/shard_map/place_pieces/pallas_call | solution.py:306
  (125 shorter events, 42.5 us)
Async XLA Ops:
  0.6 19.2 %collective-permute-start = (bf16[4,128,640]{2,1,0:T(8,128)(2,1)}, bf16[4,128,640]{2,1,0:T(8,128)(2,1)S(1)}, u32[]{:S(2)}, u32[]{:S(2)}) collective-permute-start(bf16[4,128,640]{2,1,0:T(8,128)(2,1)} %x0.2), channel_id=1, source_target_pairs={{0,1},{1,0},{2,3},{3,2},{4,5},{5,4},{6,7},{7,6},{8,9},{9,8},{10,11... | collective-permute-start | bytes 1966088 | tf_op jit(solution)/shard_map/ppermute | solution.py:31
  5.1 32.4 %collective-permute-start.2 = (bf16[4,128,640]{2,1,0:T(8,128)(2,1)}, bf16[4,128,640]{2,1,0:T(8,128)(2,1)S(1)}, u32[]{:S(2)}, u32[]{:S(2)}) collective-permute-start(bf16[4,128,640]{2,1,0:T(8,128)(2,1)} %x0.2), channel_id=1, source_target_pairs={{0,2},{1,3},{2,4},{3,5},{4,6},{5,7},{6,0},{7,1},{8,10},{9,11},{10,... | collective-permute-start | bytes 1966088 | tf_op jit(solution)/shard_map/ppermute | solution.py:31
  19.8 18.8 %collective-permute-start.4 = (bf16[4,128,640]{2,1,0:T(8,128)(2,1)S(1)}, bf16[4,128,640]{2,1,0:T(8,128)(2,1)S(1)}, u32[]{:S(2)}, u32[]{:S(2)}) collective-permute-start(bf16[4,128,640]{2,1,0:T(8,128)(2,1)S(1)} %collective-permute-done.x1), channel_id=1, source_target_pairs={{0,6},{1,7},{2,0},{3,1},{4,2},{5,3},{6,4},{7,5},{8,14},{9,15},{10,... | collective-permute-start | bytes 1966088 | tf_op jit(solution)/shard_map/ppermute | solution.py:31
  30.9 24.9 %collective-permute-start.20 = (bf16[128,16,256]{2,1,0:T(8,128)(2,1)}, bf16[128,16,256]{2,1,0:T(8,128)(2,1)S(1)}, u32[]{:S(2)}, u32[]{:S(2)}) collective-permute-start(bf16[128,16,256]{2,1,0:T(8,128)(2,1)} %get-tuple-element.42), channel_id=1, source_target_pairs={{0,32},{8,40},{16,48},{24,56},{32,0},{40,8},{48,16},{56,24},{64,96... | collective-permute-start | bytes 3145736 | tf_op jit(solution)/shard_map/ppermute | solution.py:41
  36.4 57.7 %collective-permute-start.13 = (bf16[256,16,256]{2,1,0:T(8,128)(2,1)}, bf16[256,16,256]{2,1,0:T(8,128)(2,1)}, u32[]{:S(2)}, u32[]{:S(2)}) collective-permute-start(bf16[256,16,256]{2,1,0:T(8,128)(2,1)} %get-tuple-element.30), channel_id=1, source_target_pairs={{0,64},{8,72},{16,80},{24,88},{32,96},{40,104},{48,112},{56,120},{... | collective-permute-start | bytes 6291464 | tf_op jit(solution)/shard_map/ppermute | solution.py:41
  37.1 21.2 %collective-permute-start.1 = (bf16[4,128,640]{2,1,0:T(8,128)(2,1)S(1)}, bf16[4,128,640]{2,1,0:T(8,128)(2,1)S(1)}, u32[]{:S(2)}, u32[]{:S(2)}) collective-permute-start(bf16[4,128,640]{2,1,0:T(8,128)(2,1)S(1)} %copy-done), channel_id=1, source_target_pairs={{0,6},{1,7},{2,0},{3,1},{4,2},{5,3},{6,4},{7,5},{8,14},{9,15},{10,... | collective-permute-start | bytes 1966088 | tf_op jit(solution)/shard_map/ppermute | solution.py:31
  37.6 21.3 %collective-permute-start.3 = (bf16[4,128,640]{2,1,0:T(8,128)(2,1)S(1)}, bf16[4,128,640]{2,1,0:T(8,128)(2,1)S(1)}, u32[]{:S(2)}, u32[]{:S(2)}) collective-permute-start(bf16[4,128,640]{2,1,0:T(8,128)(2,1)S(1)} %collective-permute-done.2.x3), channel_id=1, source_target_pairs={{0,2},{1,3},{2,4},{3,5},{4,6},{5,7},{6,0},{7,1},{8,10},{9,11},{10,... | collective-permute-start | bytes 1966088 | tf_op jit(solution)/shard_map/ppermute | solution.py:31
  38.6 27.1 %collective-permute-start.5 = (bf16[4,128,640]{2,1,0:T(8,128)(2,1)S(1)}, bf16[4,128,640]{2,1,0:T(8,128)(2,1)S(1)}, u32[]{:S(2)}, u32[]{:S(2)}) collective-permute-start(bf16[4,128,640]{2,1,0:T(8,128)(2,1)S(1)} %collective-permute-done.x1), channel_id=1, source_target_pairs={{0,2},{1,3},{2,4},{3,5},{4,6},{5,7},{6,0},{7,1},{8,10},{9,11},{10,... | collective-permute-start | bytes 1966088 | tf_op jit(solution)/shard_map/ppermute | solution.py:31
  55.8 36.9 %collective-permute-start.23 = (bf16[128,16,256]{2,1,0:T(8,128)(2,1)}, bf16[128,16,256]{2,1,0:T(8,128)(2,1)}, u32[]{:S(2)}, u32[]{:S(2)}) collective-permute-start(bf16[128,16,256]{2,1,0:T(8,128)(2,1)} %get-tuple-element.40.refs_0_), channel_id=1, source_target_pairs={{0,8},{8,0},{16,24},{24,16},{32,40},{40,32},{48,56},{56,48},{64,72... | collective-permute-start | bytes 3145736 | tf_op jit(solution)/shard_map/ppermute | solution.py:41
  58.9 33.9 %collective-permute-start.21 = (bf16[128,16,256]{2,1,0:T(8,128)(2,1)}, bf16[128,16,256]{2,1,0:T(8,128)(2,1)}, u32[]{:S(2)}, u32[]{:S(2)}) collective-permute-start(bf16[128,16,256]{2,1,0:T(8,128)(2,1)} %get-tuple-element.43), channel_id=1, source_target_pairs={{0,16},{8,24},{16,32},{24,40},{32,48},{40,56},{48,0},{56,8},{64,80... | collective-permute-start | bytes 3145736 | tf_op jit(solution)/shard_map/ppermute | solution.py:41
  65.6 28.2 %collective-permute-start.22 = (bf16[128,16,256]{2,1,0:T(8,128)(2,1)}, bf16[128,16,256]{2,1,0:T(8,128)(2,1)}, u32[]{:S(2)}, u32[]{:S(2)}) collective-permute-start(bf16[128,16,256]{2,1,0:T(8,128)(2,1)} %get-tuple-element.45), channel_id=1, source_target_pairs={{0,48},{8,56},{16,0},{24,8},{32,16},{40,24},{48,32},{56,40},{64,11... | collective-permute-start | bytes 3145736 | tf_op jit(solution)/shard_map/ppermute | solution.py:41
  92.7 16.8 %collective-permute-start.8 = (bf16[2,256,640]{2,1,0:T(8,128)(2,1)}, bf16[2,256,640]{2,1,0:T(8,128)(2,1)}, u32[]{:S(2)}, u32[]{:S(2)}) collective-permute-start(bf16[2,256,640]{2,1,0:T(8,128)(2,1)} %get-tuple-element.27), channel_id=1, source_target_pairs={{0,2},{1,3},{2,4},{3,5},{4,6},{5,7},{6,0},{7,1},{8,10},{9,11},{10,... | collective-permute-start | bytes 1966088 | tf_op jit(solution)/shard_map/ppermute | solution.py:31
  92.8 36.0 %collective-permute-start.25 = (bf16[128,16,256]{2,1,0:T(8,128)(2,1)}, bf16[128,16,256]{2,1,0:T(8,128)(2,1)S(1)}, u32[]{:S(2)}, u32[]{:S(2)}) collective-permute-start(bf16[128,16,256]{2,1,0:T(8,128)(2,1)} %copy-done.10), channel_id=1, source_target_pairs={{0,8},{8,0},{16,24},{24,16},{32,40},{40,32},{48,56},{56,48},{64,72... | collective-permute-start | bytes 3145736 | tf_op jit(solution)/shard_map/ppermute | solution.py:41
  93.8 35.6 %collective-permute-start.24 = (bf16[128,16,256]{2,1,0:T(8,128)(2,1)}, bf16[128,16,256]{2,1,0:T(8,128)(2,1)S(1)}, u32[]{:S(2)}, u32[]{:S(2)}) collective-permute-start(bf16[128,16,256]{2,1,0:T(8,128)(2,1)} %collective-permute-done.21.refs_1_), channel_id=1, source_target_pairs={{0,8},{8,0},{16,24},{24,16},{32,40},{40,32},{48,56},{56,48},{64,72... | collective-permute-start | bytes 3145736 | tf_op jit(solution)/shard_map/ppermute | solution.py:41
  94.1 38.3 %collective-permute-start.26 = (bf16[128,16,256]{2,1,0:T(8,128)(2,1)}, bf16[128,16,256]{2,1,0:T(8,128)(2,1)}, u32[]{:S(2)}, u32[]{:S(2)}) collective-permute-start(bf16[128,16,256]{2,1,0:T(8,128)(2,1)} %collective-permute-done.22.refs_3_), channel_id=1, source_target_pairs={{0,8},{8,0},{16,24},{24,16},{32,40},{40,32},{48,56},{56,48},{64,72... | collective-permute-start | bytes 3145736 | tf_op jit(solution)/shard_map/ppermute | solution.py:41
  107.0 32.3 %collective-permute-start.19 = (bf16[128,16,256]{2,1,0:T(8,128)(2,1)}, bf16[128,16,256]{2,1,0:T(8,128)(2,1)}, u32[]{:S(2)}, u32[]{:S(2)}) collective-permute-start(bf16[128,16,256]{2,1,0:T(8,128)(2,1)} %get-tuple-element.38), channel_id=1, source_target_pairs={{0,16},{8,24},{16,32},{24,40},{32,48},{40,56},{48,0},{56,8},{64,80... | collective-permute-start | bytes 3145736 | tf_op jit(solution)/shard_map/ppermute | solution.py:41
  109.6 29.7 %collective-permute-start.27 = (bf16[128,16,256]{2,1,0:T(8,128)(2,1)}, bf16[128,16,256]{2,1,0:T(8,128)(2,1)}, u32[]{:S(2)}, u32[]{:S(2)}) collective-permute-start(bf16[128,16,256]{2,1,0:T(8,128)(2,1)} %get-tuple-element.46), channel_id=1, source_target_pairs={{0,48},{8,56},{16,0},{24,8},{32,16},{40,24},{48,32},{56,40},{64,11... | collective-permute-start | bytes 3145736 | tf_op jit(solution)/shard_map/ppermute | solution.py:41
  128.8 25.4 %collective-permute-start.14 = (bf16[2,256,640]{2,1,0:T(8,128)(2,1)}, bf16[2,256,640]{2,1,0:T(8,128)(2,1)}, u32[]{:S(2)}, u32[]{:S(2)}) collective-permute-start(bf16[2,256,640]{2,1,0:T(8,128)(2,1)} %get-tuple-element.36), channel_id=1, source_target_pairs={{0,6},{1,7},{2,0},{3,1},{4,2},{5,3},{6,4},{7,5},{8,14},{9,15},{10,... | collective-permute-start | bytes 1966088 | tf_op jit(solution)/shard_map/ppermute | solution.py:31
  129.4 24.7 %collective-permute-start.15 = (bf16[2,256,640]{2,1,0:T(8,128)(2,1)}, bf16[2,256,640]{2,1,0:T(8,128)(2,1)}, u32[]{:S(2)}, u32[]{:S(2)}) collective-permute-start(bf16[2,256,640]{2,1,0:T(8,128)(2,1)} %get-tuple-element.37), channel_id=1, source_target_pairs={{0,2},{1,3},{2,4},{3,5},{4,6},{5,7},{6,0},{7,1},{8,10},{9,11},{10,... | collective-permute-start | bytes 1966088 | tf_op jit(solution)/shard_map/ppermute | solution.py:31
  132.4 17.9 %collective-permute-start.10 = (bf16[256,640]{1,0:T(8,128)(2,1)}, bf16[256,640]{1,0:T(8,128)(2,1)}, u32[]{:S(2)}, u32[]{:S(2)}) collective-permute-start(bf16[256,640]{1,0:T(8,128)(2,1)} %get-tuple-element.49), channel_id=1, source_target_pairs={{0,6},{1,7},{2,0},{3,1},{4,2},{5,3},{6,4},{7,5},{8,14},{9,15},{10,... | collective-permute-start | bytes 983048 | tf_op jit(solution)/shard_map/ppermute | solution.py:31
  139.3 26.6 %collective-permute-start.28 = (bf16[128,16,256]{2,1,0:T(8,128)(2,1)}, bf16[128,16,256]{2,1,0:T(8,128)(2,1)}, u32[]{:S(2)}, u32[]{:S(2)}) collective-permute-start(bf16[128,16,256]{2,1,0:T(8,128)(2,1)} %get-tuple-element.47), channel_id=1, source_target_pairs={{0,32},{8,40},{16,48},{24,56},{32,0},{40,8},{48,16},{56,24},{64,96... | collective-permute-start | bytes 3145736 | tf_op jit(solution)/shard_map/ppermute | solution.py:41
  157.2 23.2 %collective-permute-start.29 = (bf16[128,16,256]{2,1,0:T(8,128)(2,1)}, bf16[128,16,256]{2,1,0:T(8,128)(2,1)}, u32[]{:S(2)}, u32[]{:S(2)}) collective-permute-start(bf16[128,16,256]{2,1,0:T(8,128)(2,1)} %get-tuple-element.33.refs_0_), channel_id=1, source_target_pairs={{0,8},{8,0},{16,24},{24,16},{32,40},{40,32},{48,56},{56,48},{64,72... | collective-permute-start | bytes 3145736 | tf_op jit(solution)/shard_map/ppermute | solution.py:41
  160.9 19.6 %collective-permute-start.30 = (bf16[128,16,256]{2,1,0:T(8,128)(2,1)}, bf16[128,16,256]{2,1,0:T(8,128)(2,1)}, u32[]{:S(2)}, u32[]{:S(2)}) collective-permute-start(bf16[128,16,256]{2,1,0:T(8,128)(2,1)} %collective-permute-done.19.refs_1_), channel_id=1, source_target_pairs={{0,8},{8,0},{16,24},{24,16},{32,40},{40,32},{48,56},{56,48},{64,72... | collective-permute-start | bytes 3145736 | tf_op jit(solution)/shard_map/ppermute | solution.py:41
  163.2 17.3 %collective-permute-start.32 = (bf16[128,16,256]{2,1,0:T(8,128)(2,1)}, bf16[128,16,256]{2,1,0:T(8,128)(2,1)}, u32[]{:S(2)}, u32[]{:S(2)}) collective-permute-start(bf16[128,16,256]{2,1,0:T(8,128)(2,1)} %collective-permute-done.27.refs_3_), channel_id=1, source_target_pairs={{0,8},{8,0},{16,24},{24,16},{32,40},{40,32},{48,56},{56,48},{64,72... | collective-permute-start | bytes 3145736 | tf_op jit(solution)/shard_map/ppermute | solution.py:41
  (32 other events, 529.9 us)

commit v2 on v1

--- a/solution.py
+++ b/solution.py
@@ -42,7 +42,7 @@
 
 
 def decode_kernel(
-    rows, first_row, sources, targets, table, x0, x1, x2, x3, x4, x5, x6, x7, gain, wq, wk, wv, wo, pool,
+    rows, first_row, where, table, x0, x1, x2, x3, x4, x5, x6, x7, gain, wq, wk, wv, wo, pool,
     lane_row, query_gain, key_gain, plus, minus, local,
     x_v, wq_v, wk_v, wv_v, wo_v, pool_v, qkv, ctx, out_v, sems,
 ):
@@ -53,7 +53,7 @@
     xs = (x0, x1, x2, x3, x4, x5, x6, x7)
     w_copies, o_copies = [], []
     for k in range(8):
-        span = pl.ds(pl.multiple_of(sources[k] * width, width), width)
+        span = pl.ds(pl.multiple_of(where[k] * width, width), width)
         w_copies.append(
             (
                 pltpu.make_async_copy(wq.at[span], wq_v.at[k], sems.at[0, k]),
@@ -61,7 +61,7 @@
                 pltpu.make_async_copy(wv.at[span], wv_v.at[k], sems.at[2, k]),
             )
         )
-        span = pl.ds(pl.multiple_of(targets[k] * width, 128), width)
+        span = pl.ds(pl.multiple_of(where[8 + k] * width, 128), width)
         o_copies.append(pltpu.make_async_copy(wo.at[:, span], wo_v.at[k], sems.at[3, k]))
     pool_copy = pltpu.make_async_copy(pool, pool_v, sems.at[4, 0])
     x_copies = [
@@ -86,7 +86,7 @@
     for k in range(8):
         for copy in w_copies[k]:
             copy.wait()
-        normed = x_v[k].reshape(count, width).astype(jnp.float32) * inverse * gain[sources[k]]
+        normed = x_v[k].reshape(count, width).astype(jnp.float32) * inverse * gain[where[k]].astype(jnp.float32)
         normed = normed.astype(jnp.bfloat16)
         q_part = jnp.dot(normed, wq_v[k], preferred_element_type=jnp.float32)
         k_part = jnp.dot(normed, wk_v[k], preferred_element_type=jnp.float32)
@@ -103,7 +103,7 @@
         lanes = slice(head * HEAD, (head + 1) * HEAD)
         raw = qkv[:, lanes]
         mean = jnp.mean(raw * raw, axis=1, keepdims=True)
-        head_gain = query_gain[...] if head < 4 else key_gain[...]
+        head_gain = (query_gain if head < 4 else key_gain)[...].astype(jnp.float32)
         qkv[:, lanes] = raw * lax.rsqrt(mean + EPSILON) * head_gain
 
     pool_copy.wait()
@@ -130,12 +130,12 @@
         ).astype(jnp.bfloat16)
         fresh_k = jnp.concatenate(tiles(4), axis=0).astype(jnp.bfloat16)
         fresh_v = jnp.concatenate(tiles(5), axis=0).astype(jnp.bfloat16)
-        blocks = [pool_v[table[i * (GROUP * 6) + j]] for j in range(GROUP * 6)]
+        blocks = [pool_v[table[first_row * 6 + i * (GROUP * 6) + j]] for j in range(GROUP * 6)]
         cached_k = jnp.concatenate([b[:, :HEAD] for b in blocks], axis=0)
         cached_v = jnp.concatenate([b[:, HEAD:] for b in blocks], axis=0)
         scores = lax.dot_general(queries, cached_k, contract_last, preferred_element_type=jnp.float32)
         fresh = lax.dot_general(queries, fresh_k, contract_last, preferred_element_type=jnp.float32)
-        scores = jnp.where(lane_row[i] == query_row, scores * scale, NEG)
+        scores = jnp.where(lane_row[first_row // GROUP + i] == query_row, scores * scale, NEG)
         fresh = jnp.where(fresh_ok, fresh * scale, NEG)
         top = jnp.maximum(
             jnp.max(scores, axis=1, keepdims=True), jnp.max(fresh, axis=1, keepdims=True)
@@ -174,7 +174,7 @@
 
 
 def decode(
-    rows, first_row, sources, targets, table, xs, gain, wq, wk, wv, wo, pool, lane_row, query_gain, key_gain
+    rows, first_row, where, table, xs, gain, wq, wk, wv, wo, pool, lane_row, query_gain, key_gain
 ):
     steps, _, width = xs[0].shape
     count = steps * rows
@@ -189,7 +189,7 @@
             jax.ShapeDtypeStruct((2, count, width), bf16),
             jax.ShapeDtypeStruct((4, count, width), bf16),
         ),
-        in_specs=[smem] * 3 + [hbm] * 8 + [vmem] + [hbm] * 5 + [vmem] * 3,
+        in_specs=[smem] * 2 + [hbm] * 8 + [vmem] + [hbm] * 5 + [vmem] * 3,
         out_specs=(hbm, hbm, hbm),
         scratch_shapes=[
             pltpu.VMEM((8, steps, rows, width), bf16),
@@ -208,14 +208,16 @@
             flops=2 * count * 5120 * 1280, bytes_accessed=24 * MIB, transcendentals=0
         ),
         name="decode_rows",
-    )(sources, targets, table, *xs, gain, wq, wk, wv, wo, pool, lane_row, query_gain, key_gain)
+    )(where, table, *xs, gain, wq, wk, wv, wo, pool, lane_row, query_gain, key_gain)
 
 
 def slots_kernel(table, order, blocks, *refs):
     outs, (blocks_v, sems) = refs[:-7], refs[-2:]
     stages = refs[-7:-2]
-    load = pltpu.make_async_copy(blocks, blocks_v, sems.at[0])
+    count = blocks.shape[0]
+    load = pltpu.make_async_copy(blocks, blocks_v.at[pl.ds(0, count)], sems.at[0])
     load.start()
+    blocks_v[count] = jnp.zeros(blocks.shape[1:], blocks.dtype)
     load.wait()
     copies = []
     if len(outs) == 5:
@@ -224,18 +226,16 @@
             stages[4][m] = blocks_v[order[m]]
             return carry
 
-        lax.fori_loop(0, outs[4].shape[0], pick, 0, unroll=8)
+        lax.fori_loop(0, outs[4].shape[0], pick, 0, unroll=16)
         copies.append(pltpu.make_async_copy(stages[4], outs[4], sems.at[5]))
         copies[0].start()
     for d in (2, 1, 3, 0):
 
         def one(j, carry):
-            at = table[d * 2 * CAP + j]
-            block = blocks_v[jnp.maximum(at, 0)]
-            stages[d][j] = jnp.where(at >= 0, block, jnp.zeros_like(block))
+            stages[d][j] = blocks_v[table[d * 2 * CAP + j]]
             return carry
 
-        lax.fori_loop(0, 2 * CAP, one, 0, unroll=8)
+        lax.fori_loop(0, 2 * CAP, one, 0, unroll=16)
         copies.append(pltpu.make_async_copy(stages[d], outs[d], sems.at[1 + d]))
         copies[-1].start()
     for copy in copies:
@@ -255,7 +255,7 @@
         scratch_shapes=[pltpu.VMEM((2 * CAP,) + tail, blocks.dtype)] * 4
         + [
             pltpu.VMEM((order.shape[0],) + tail, blocks.dtype),
-            pltpu.VMEM(blocks.shape, blocks.dtype),
+            pltpu.VMEM((blocks.shape[0] + 1,) + tail, blocks.dtype),
             pltpu.SemaphoreType.DMA((6,)),
         ],
         compiler_params=pltpu.CompilerParams(vmem_limit_bytes=60 * MIB),
@@ -264,7 +264,7 @@
     )(table, order, blocks)
 
 
-def slot_table(target, values, own_z, own_x, own_c):
+def slot_table(target, values, empty, own_z, own_x, own_c):
     order = jnp.arange(target.shape[0], dtype=jnp.int32)
     earlier = (target[:, None] == target[None, :]) & (order[None, :] < order[:, None])
     rank = jnp.sum(earlier.astype(jnp.int32), axis=1)
@@ -272,59 +272,60 @@
     far, other = slot // (2 * CAP), (slot // CAP) % 2
     wanted = own_z * 8 + ((own_x + far) % 4) * 2 + (own_c + other) % 2
     match = (wanted * CAP + slot % CAP)[:, None] == (target * CAP + rank)[None, :]
-    return jnp.max(jnp.where(match, values[None, :], -1), axis=1)
+    return jnp.min(jnp.where(match, values[None, :], empty), axis=1)
 
 
 def cross(received):
-    return received + [inst_move(r, 0, 0, 1) for r in received]
-
-
-def place_kernel(places_ref, *refs):
-    pieces, out, stage, sems = refs[:8], refs[-3], refs[-2], refs[-1]
+    return inst_move(jnp.concatenate([r[CAP:] for r in received]), 0, 0, 1)
+
+
+def place_kernel(offsets, places_ref, *refs):
+    count = len(offsets)
+    arrays, out, stage, sems = refs[: max(offsets)[0] + 1], refs[-3], refs[-2], refs[-1]
     ins, outs = [], []
-    for j in range(8):
+    for j, (which, offset) in enumerate(offsets):
         start = pl.multiple_of(places_ref[j] * CAP, CAP)
-        part = pieces[j].at[pl.ds((j // 4) * CAP, CAP)]
+        part = arrays[which].at[pl.ds(offset * CAP, CAP)]
         ins.append(pltpu.make_async_copy(part, stage.at[j], sems.at[0, j]))
         outs.append(pltpu.make_async_copy(stage.at[j], out.at[pl.ds(start, CAP)], sems.at[1, j]))
     for copy in ins:
         copy.start()
-    for j in range(8):
+    for j in range(count):
         ins[j].wait()
         outs[j].start()
     for copy in outs:
         copy.wait()
 
 
-def place_pieces(where, pieces, before):
+def place_pieces(where, arrays, offsets, before):
     smem = pl.BlockSpec(memory_space=pltpu.SMEM)
     either = pl.BlockSpec(memory_space=pl.ANY)
     hbm = pl.BlockSpec(memory_space=pltpu.HBM)
-    blocks = pieces[0].shape[1:]
-    shape = jax.ShapeDtypeStruct((16 * CAP,) + blocks, pieces[0].dtype)
+    blocks = arrays[0].shape[1:]
+    shape = jax.ShapeDtypeStruct((16 * CAP,) + blocks, arrays[0].dtype)
     extra = [] if before is None else [before]
     return pl.pallas_call(
-        place_kernel,
+        functools.partial(place_kernel, tuple(offsets)),
         out_shape=shape,
-        in_specs=[smem] + [either] * 8 + [hbm] * len(extra),
+        in_specs=[smem] + [either] * len(arrays) + [hbm] * len(extra),
         out_specs=hbm,
         scratch_shapes=[
-            pltpu.VMEM((8, CAP) + blocks, pieces[0].dtype),
-            pltpu.SemaphoreType.DMA((2, 8)),
+            pltpu.VMEM((len(offsets), CAP) + blocks, arrays[0].dtype),
+            pltpu.SemaphoreType.DMA((2, len(offsets))),
         ],
-        input_output_aliases={} if before is None else {9: 0},
+        input_output_aliases={} if before is None else {1 + len(arrays): 0},
         compiler_params=pltpu.CompilerParams(vmem_limit_bytes=60 * MIB),
         cost_estimate=pl.CostEstimate(flops=0, bytes_accessed=16 * MIB, transcendentals=0),
         name="place_pieces",
-    )(where, *pieces, *extra)
+    )(where, *arrays, *extra)
 
 
 def after(array, *others):
     return lax.optimization_barrier((array,) + others)[0]
 
 
-def gather_rows(x):
-    other = tp_move(x, 0, 1)
+def gather_rows(x, first):
+    other = after(tp_move(x, 0, 1), *first)
     up, down = tp_move(x, 3, 0), tp_move(x, 1, 0)
     other_up, other_down = tp_move(other, 3, 0), tp_move(other, 1, 0)
     far = tp_move(down, 1, 0)
@@ -332,12 +333,17 @@
     return [x, other, up, down, far, other_up, other_down, other_far]
 
 
-def scatter_sum(plus, minus, local):
+def scatter_first(plus, minus, local):
     f32, bf16 = jnp.float32, jnp.bfloat16
     below = tp_move(plus, 1, 0)
     above = tp_move(minus, 3, 0)
     up = (local[0].astype(f32) + below[0].astype(f32)).astype(bf16)
     down = (local[1].astype(f32) + above[0].astype(f32)).astype(bf16)
+    return below, above, up, down
+
+
+def scatter_rest(local, below, above, up, down):
+    f32, bf16 = jnp.float32, jnp.bfloat16
     from_below = tp_move(up, 1, 0)
     from_above = tp_move(down, 3, 0)
     other = (local[3].astype(f32) + below[1].astype(f32) + from_above.astype(f32)).astype(bf16)
@@ -362,66 +368,80 @@
     move_target,
 ):
     step_count, row_count, width = inputs.shape
-    f32 = jnp.float32
     own = lax.axis_index("inst")
     own_z, own_x, own_c = own // 8, (own // 2) % 4, own % 2
 
     target = move_target[:, 0]
     other_target = inst_move(target, 1, 0, 0)
 
+    table = slot_table(target, move_block, kv_pool.shape[0], own_z, own_x, own_c)
+    *slots, compact = fill_slots(table, move_block, kv_pool, True)
+
     rows = row_count // CHUNKS
-    gathered = gather_rows(inputs)
-
-    table = slot_table(target, move_block, own_z, own_x, own_c)
-    table = after(table, gathered[1])
-    *slots, compact = fill_slots(table, move_block, kv_pool, True)
-    compact = after(compact, other_target)
+    gathered = gather_rows(inputs, (compact, other_target))
+    compact = after(compact, *gathered[1:4])
     other_target = after(other_target, compact)
     other_blocks = inst_move(compact, 1, 0, 0)
     far = inst_move(slots[2], 0, 2, 0)
-    near = inst_move(after(slots[1], far, gathered[5]), 0, 1, 0)
-    back = inst_move(after(slots[3], far, gathered[5]), 0, 3, 0)
+    near = inst_move(after(slots[1], far, *gathered), 0, 1, 0)
+    back = inst_move(after(slots[3], far, *gathered), 0, 3, 0)
     order = jnp.arange(move_block.shape[0], dtype=jnp.int32)
-    other_table = slot_table(other_target, order, own_z, own_x, own_c)
-
-    gain = norm_gain.astype(f32).reshape(8, 1, width)
+    other_table = slot_table(other_target, order, order.shape[0], own_z, own_x, own_c)
+
+    gain = norm_gain.reshape(8, 1, width)
     positions = jnp.arange(block_table.shape[1] * PAGE, dtype=jnp.int32)
     lane_row = jnp.where(
         positions[None, :] < cache_len[:, None],
         (jnp.arange(row_count, dtype=jnp.int32) % GROUP)[:, None],
         -1,
     ).reshape(row_count // GROUP, 1, -1)
-    sources, targets = places(GATHERED), places(SCATTERED)
-    query_gain = query_gain.astype(f32).reshape(1, HEAD)
-    key_gain = key_gain.astype(f32).reshape(1, HEAD)
+    tp_where = places(GATHERED + SCATTERED)
+    query_gain = query_gain.reshape(1, HEAD)
+    key_gain = key_gain.reshape(1, HEAD)
+    blocks_of_rows = block_table.reshape(-1)
     def where(z):
         return jnp.stack(
             [z * 8 + ((own_x - j % 4) % 4) * 2 + (own_c + j // 4) % 2 for j in range(8)]
         ).astype(jnp.int32)
 
-    arrived = place_pieces(where(own_z), cross([slots[0], near, far, back]), None)
-
-    chunks = []
-    for c in range(CHUNKS):
-        first = c * rows
-        tables = block_table[first : first + rows].reshape(-1)
-        lanes = lane_row[first // GROUP : (first + rows) // GROUP]
-        if c == 1:
-            other_table = after(other_table, parts[0])
-            other_slots = fill_slots(other_table, order, other_blocks, False)
-            other_near = inst_move(other_slots[1], 0, 1, 0)
-            other_back = inst_move(other_slots[3], 0, 3, 0)
-            gathered[0] = after(gathered[0], other_slots[0])
-        parts = decode(
-            rows, first, sources, targets, tables, gathered, gain, query_weight, key_weight,
-            value_weight, output_weight, kv_pool, lanes, query_gain, key_gain,
+
+    def decode_part(c):
+        return decode(
+            rows, c * rows, tp_where, blocks_of_rows, gathered, gain, query_weight, key_weight,
+            value_weight, output_weight, kv_pool, lane_row, query_gain, key_gain,
         )
-        chunks.append(scatter_sum(*parts).reshape(step_count, rows, width))
-    mixed_out = jnp.concatenate(chunks, axis=1)
-
-    other_far = inst_move(after(other_slots[2], arrived, other_near, other_back), 0, 2, 0)
-    other_pieces = cross([other_slots[0], other_near, other_far, other_back])
-    arrived = place_pieces(where(1 - own_z), other_pieces, arrived)
+
+    plus, minus, local = decode_part(0)
+    sums = scatter_first(plus, minus, local)
+    other_table = after(other_table, near, back, plus)
+    other_slots = fill_slots(other_table, order, other_blocks, False)
+    other_far = inst_move(other_slots[2], 0, 2, 0)
+    gathered[0] = after(gathered[0], other_slots[0])
+    later_parts = decode_part(1)
+    later_sums = scatter_first(*later_parts)
+    chunks = [scatter_rest(local, *sums), scatter_rest(later_parts[2], *later_sums)]
+    mixed_out = jnp.concatenate(
+        [chunk.reshape(step_count, rows, width) for chunk in chunks], axis=1
+    )
+
+    def where(z, far_xs, cores):
+        return jnp.stack(
+            [z * 8 + ((own_x - dx) % 4) * 2 + (own_c + dc) % 2 for dc in cores for dx in far_xs]
+        ).astype(jnp.int32)
+
+    other_near = inst_move(after(other_slots[1], other_far, later_parts[0]), 0, 1, 0)
+    other_back = inst_move(after(other_slots[3], other_far, later_parts[0]), 0, 3, 0)
+    pieces = [slots[0], near, far, back]
+    pieces.append(cross(after(pieces, later_parts[0])))
+    offsets = [(j, 0) for j in range(4)] + [(4, j) for j in range(4)]
+    arrived = place_pieces(where(own_z, (0, 1, 2, 3), (0, 1)), pieces, offsets, None)
+    pieces = [other_slots[0], other_far]
+    pieces.append(cross(after(pieces, later_parts[0])))
+    offsets = [(0, 0), (1, 0), (2, 0), (2, 1)]
+    arrived = place_pieces(where(1 - own_z, (0, 2), (0, 1)), pieces, offsets, arrived)
+    pieces = [other_near, other_back]
+    pieces.append(cross(pieces))
+    arrived = place_pieces(where(1 - own_z, (1, 3), (0, 1)), pieces, offsets, arrived)
     return (mixed_out, arrived)
 
 

time: 186 us -> 170 us (0.914)
  waiting for transfers between devices: 63.1 us -> 40.9 us
  other arithmetic: 14.4 us -> 20 us
  starting transfers between devices: 47.6 us -> 44.1 us
  local copies, waits for them, and re-layouts: 7.95 us -> 11.4 us
    ppermute x17, waiting for transfers between devices: 43.9 us -> 29.5 us  [tp_move(): return lax.ppermute(array, 'tp', pairs)]
    ppermute x16 -> x11, waiting for transfers between devices: 19.2 us -> 11.4 us  [inst_move(): return lax.ppermute(array, 'inst', pairs)]
    ppermute x16 -> x11, starting transfers between devices: 24.8 us -> 19.7 us  [inst_move(): return lax.ppermute(array, 'inst', pairs)]
    concatenate x1 -> x4, other arithmetic: 0.89 us -> 4.64 us  [the longest x3 3.75 us: cross(): return inst_move(jnp.concatenate([r[CAP:] for r in received]), 0, 0, 1)]
    unnamed x46 -> x41, local copies, waits for them, and re-layouts: 1.73 us -> 4.29 us
    reduce_min x0 -> x2, other arithmetic: none -> 2.32 us  [slot_table(): return jnp.min(jnp.where(match, values[None, :], empty), axis=1)]
    reduce_max x2 -> x0, other arithmetic: 2.32 us -> none  [slot_table(): return jnp.max(jnp.where(match, values[None, :], -1), axis=1)]
    pallas_call x2 -> x3, Pallas kernels: 8.62 us -> 10.4 us  [place_pieces(): pl.pallas_call(functools.partial(place_kernel, tuple(offsets)), out_shape...]
  transfers between devices with their start and end apart: 33 -> 28, of which waited for: 9 -> 9; matrix products, arithmetic and copies ran while one was open for 11% -> 16% of each run, Pallas kernels for 25% -> 26%
where the time goes in v2:
time: 170 us
  Pallas kernels  52.2 us (31%)
  starting transfers between devices  44.1 us (26%)
  waiting for transfers between devices  40.9 us (24%)
  other arithmetic  20 us (12%)
  local copies, waits for them, and re-layouts  11.4 us (7%)
    pallas_call x2, Pallas kernels, decode(): pl.pallas_call(functools.partial(decode_kernel, rows, first_row), out_sha...  30.5 us
    ppermute x17, waiting for transfers between devices, tp_move(): return lax.ppermute(array, 'tp', pairs)  29.5 us
    ppermute x17, starting transfers between devices, tp_move(): return lax.ppermute(array, 'tp', pairs)  24.4 us
    ppermute x11, starting transfers between devices, inst_move(): return lax.ppermute(array, 'inst', pairs)  19.7 us
    ppermute x11, waiting for transfers between devices, inst_move(): return lax.ppermute(array, 'inst', pairs)  11.4 us
    pallas_call x2, Pallas kernels, fill_slots(): pl.pallas_call(slots_kernel, out_shape=tuple((jax.ShapeDtypeStruct((n,) +...  11.3 us
    pallas_call x3, Pallas kernels, place_pieces(): pl.pallas_call(functools.partial(place_kernel, tuple(offsets)), out_shape...  10.4 us
    unnamed x41, local copies, waits for them, and re-layouts  4.29 us
  transfers between devices with their start and end apart: 28, of which 9 were waited for; matrix products, arithmetic and copies ran while one was open for 16% of the time, Pallas kernels for 26%

profile of v2, /device:TPU:1, one launch (start us, length us, event | category | flops | bytes accessed | tf_op | source)
XLA Modules:
  0.0 169.7 jit_solution(2719623771669749098)
XLA Ops:
  0.6 4.5 %collective-permute-start = (bf16[4,128,640]{2,1,0:T(8,128)(2,1)}, bf16[4,128,640]{2,1,0:T(8,128)(2,1)S(1)}, u32[]{:S(2)}, u32[]{:S(2)}) collective-permute-start(bf16[4,128,640]{2,1,0:T(8,128)(2,1)} %x0.2), channel_id=1, source_target_pairs={{0,1},{1,0},{2,3},{3,2},{4,5},{5,4},{6,7},{7,6},{8,9},{9,8},{10,11... | collective-permute-start | bytes 1966088 | tf_op jit(solution)/shard_map/ppermute | solution.py:31
  11.7 6.7 %fill_slots.2 = (bf16[128,16,256]{2,1,0:T(8,128)(2,1)}, bf16[128,16,256]{2,1,0:T(8,128)(2,1)}, bf16[128,16,256]{2,1,0:T(8,128)(2,1)}, bf16[128,16,256]{2,1,0:T(8,128)(2,1)}, bf16[256,16,256]{2,1,0:T(8,128)(2,1)}) custom-call(s32[512]{0:T(512)} %select_reduce_fusion.1.table, s32[256]{0:T(256)} %order.1, bf16[768,16,256]{2,1,0:T(8,128)(2,1)} %pool.3), custom_call_target="tpu_custom_call" | custom-call | bytes 16777216 | tf_op jit(solution)/shard_map/fill_slots/pallas_call | solution.py:250
  20.2 2.7 %collective-permute-start.5 = (bf16[4,128,640]{2,1,0:T(8,128)(2,1)S(1)}, bf16[4,128,640]{2,1,0:T(8,128)(2,1)S(1)}, u32[]{:S(2)}, u32[]{:S(2)}) collective-permute-start(bf16[4,128,640]{2,1,0:T(8,128)(2,1)S(1)} %collective-permute-done.x1), channel_id=1, source_target_pairs={{0,6},{1,7},{2,0},{3,1},{4,2},{5,3},{6,4},{7,5},{8,14},{9,15},{10,... | collective-permute-start | bytes 1966088 | tf_op jit(solution)/shard_map/ppermute | solution.py:31
  23.0 2.7 %collective-permute-start.13 = (bf16[128,16,256]{2,1,0:T(8,128)(2,1)}, bf16[128,16,256]{2,1,0:T(8,128)(2,1)S(1)}, u32[]{:S(2)}, u32[]{:S(2)}) collective-permute-start(bf16[128,16,256]{2,1,0:T(8,128)(2,1)} %get-tuple-element.40), channel_id=1, source_target_pairs={{0,32},{8,40},{16,48},{24,56},{32,0},{40,8},{48,16},{56,24},{64,96... | collective-permute-start | bytes 3145736 | tf_op jit(solution)/shard_map/ppermute | solution.py:41
  26.6 9.3 %collective-permute-done.5.x5 = bf16[4,128,640]{2,1,0:T(8,128)(2,1)S(1)} collective-permute-done((bf16[4,128,640]{2,1,0:T(8,128)(2,1)S(1)}, bf16[4,128,640]{2,1,0:T(8,128)(2,1)S(1)}, u32[]{:S(2)}, u32[]{:S(2)}) %collective-permute-start.5) | collective-permute-done | bytes 655392 | tf_op jit(solution)/shard_map/ppermute | solution.py:31
  35.9 3.0 %collective-permute-start.7 = (bf16[4,128,640]{2,1,0:T(8,128)(2,1)S(1)}, bf16[4,128,640]{2,1,0:T(8,128)(2,1)S(1)}, u32[]{:S(2)}, u32[]{:S(2)}) collective-permute-start(bf16[4,128,640]{2,1,0:T(8,128)(2,1)S(1)} %collective-permute-done.5.x5), channel_id=1, source_target_pairs={{0,6},{1,7},{2,0},{3,1},{4,2},{5,3},{6,4},{7,5},{8,14},{9,15},{10,... | collective-permute-start | bytes 1966088 | tf_op jit(solution)/shard_map/ppermute | solution.py:31
  38.9 8.6 %collective-permute-done.13.refs_2_ = bf16[128,16,256]{2,1,0:T(8,128)(2,1)S(1)} collective-permute-done((bf16[128,16,256]{2,1,0:T(8,128)(2,1)}, bf16[128,16,256]{2,1,0:T(8,128)(2,1)S(1)}, u32[]{:S(2)}, u32[]{:S(2)}) %collective-permute-start.13) | collective-permute-done | bytes 1048608 | tf_op jit(solution)/shard_map/ppermute | solution.py:41
  47.5 8.1 %collective-permute-done.4.x4 = bf16[4,128,640]{2,1,0:T(8,128)(2,1)S(1)} collective-permute-done((bf16[4,128,640]{2,1,0:T(8,128)(2,1)S(1)}, bf16[4,128,640]{2,1,0:T(8,128)(2,1)S(1)}, u32[]{:S(2)}, u32[]{:S(2)}) %collective-permute-start.4) | collective-permute-done | bytes 655392 | tf_op jit(solution)/shard_map/ppermute | solution.py:31
  57.6 2.4 %collective-permute-start.15 = (bf16[128,16,256]{2,1,0:T(8,128)(2,1)}, bf16[128,16,256]{2,1,0:T(8,128)(2,1)}, u32[]{:S(2)}, u32[]{:S(2)}) collective-permute-start(bf16[128,16,256]{2,1,0:T(8,128)(2,1)} %get-tuple-element.43), channel_id=1, source_target_pairs={{0,48},{8,56},{16,0},{24,8},{32,16},{40,24},{48,32},{56,40},{64,11... | collective-permute-start | bytes 3145736 | tf_op jit(solution)/shard_map/ppermute | solution.py:41
  64.4 15.3 %decode_rows.2 = (bf16[2,256,640]{2,1,0:T(8,128)(2,1)}, bf16[2,256,640]{2,1,0:T(8,128)(2,1)}, bf16[4,256,640]{2,1,0:T(8,128)(2,1)}) custom-call(s32[16]{0:T(128)} %stack.100.where, s32[768]{0:T(1024)} %reshape.198.table, bf16[4,128,640]{2,1,0:T(8,128)(2,1)} %x0.2, bf16[4,128,640]{2,1,0:T(8,128)(2,1)} %copy-done, bf16[4,128,640]{2,1,0:T(8,128)(2,1)} %copy-done.2, ...), custom_call_target="tpu_custom_call" | custom-call | flops 3355443200 | bytes 25165824 | tf_op jit(solution)/shard_map/decode_rows/pallas_call | solution.py:185
  80.7 4.6 %fill_slots.3 = (bf16[128,16,256]{2,1,0:T(8,128)(2,1)}, bf16[128,16,256]{2,1,0:T(8,128)(2,1)}, bf16[128,16,256]{2,1,0:T(8,128)(2,1)}, bf16[128,16,256]{2,1,0:T(8,128)(2,1)}) custom-call(s32[512]{0:T(512)} %select_reduce_fusion.table, s32[256]{0:T(256)} %iota.48.order, bf16[256,16,256]{2,1,0:T(8,128)(2,1)} %collective-permute-done.16.blocks), custom_call_target="tpu_custom_call" | custom-call | bytes 16777216 | tf_op jit(solution)/shard_map/fill_slots/pallas_call | solution.py:250
  88.0 15.3 %decode_rows.3 = (bf16[2,256,640]{2,1,0:T(8,128)(2,1)}, bf16[2,256,640]{2,1,0:T(8,128)(2,1)}, bf16[4,256,640]{2,1,0:T(8,128)(2,1)}) custom-call(s32[16]{0:T(128)} %stack.100.where, s32[768]{0:T(1024)} %reshape.198.table, bf16[4,128,640]{2,1,0:T(8,128)(2,1)} %x0.2, bf16[4,128,640]{2,1,0:T(8,128)(2,1)} %copy-done, bf16[4,128,640]{2,1,0:T(8,128)(2,1)} %copy-done.2, ...), custom_call_target="tpu_custom_call" | custom-call | flops 3355443200 | bytes 25165824 | tf_op jit(solution)/shard_map/decode_rows/pallas_call | solution.py:185
  111.8 5.9 %collective-permute-start.27 = (bf16[256,16,256]{2,1,0:T(8,128)(2,1)}, bf16[256,16,256]{2,1,0:T(8,128)(2,1)}, u32[]{:S(2)}, u32[]{:S(2)}) collective-permute-start(bf16[256,16,256]{2,1,0:T(8,128)(2,1)} %pad_maximum_fusion), channel_id=1, source_target_pairs={{0,8},{8,0},{16,24},{24,16},{32,40},{40,32},{48,56},{56,48},{64,72... | collective-permute-start | bytes 6291464 | tf_op jit(solution)/shard_map/ppermute | solution.py:41
  117.7 2.1 %fusion.6 = (bf16[256,640]{1,0:T(8,128)(2,1)}, bf16[256,640]{1,0:T(8,128)(2,1)}) fusion(bf16[2,256,640]{2,1,0:T(8,128)(2,1)} %collective-permute-done.9, bf16[4,256,640]{2,1,0:T(8,128)(2,1)S(1)} %copy-done.12, bf16[2,256,640]{2,1,0:T(8,128)(2,1)} %collective-permute-done.8), kind=kLoop, calls=%fused_computation.20 | loop fusion | flops 1310720 | bytes 1966080 | tf_op jit(solution)/shard_map/convert_element_type | solution.py:340
  119.8 2.1 %collective-permute-start.11 = (bf16[256,640]{1,0:T(8,128)(2,1)}, bf16[256,640]{1,0:T(8,128)(2,1)S(1)}, u32[]{:S(2)}, u32[]{:S(2)}) collective-permute-start(bf16[256,640]{1,0:T(8,128)(2,1)} %get-tuple-element.63), channel_id=1, source_target_pairs={{0,6},{1,7},{2,0},{3,1},{4,2},{5,3},{6,4},{7,5},{8,14},{9,15},{10,... | collective-permute-start | bytes 983048 | tf_op jit(solution)/shard_map/ppermute | solution.py:31
  121.9 2.2 %fusion.8 = (bf16[256,640]{1,0:T(8,128)(2,1)}, bf16[256,640]{1,0:T(8,128)(2,1)S(1)}) fusion(bf16[2,256,640]{2,1,0:T(8,128)(2,1)} %collective-permute-done.18, bf16[4,256,640]{2,1,0:T(8,128)(2,1)} %get-tuple-element.47, bf16[2,256,640]{2,1,0:T(8,128)(2,1)} %collective-permute-done.17), kind=kLoop, calls=%fused_computation.22 | loop fusion | flops 1310720 | bytes 1966080 | tf_op jit(solution)/shard_map/convert_element_type | solution.py:340
  124.0 4.1 %collective-permute-done.11 = bf16[256,640]{1,0:T(8,128)(2,1)S(1)} collective-permute-done((bf16[256,640]{1,0:T(8,128)(2,1)}, bf16[256,640]{1,0:T(8,128)(2,1)S(1)}, u32[]{:S(2)}, u32[]{:S(2)}) %collective-permute-start.11) | collective-permute-done | bytes 327712 | tf_op jit(solution)/shard_map/ppermute | solution.py:31
  128.9 3.0 %collective-permute-start.20 = (bf16[256,640]{1,0:T(8,128)(2,1)S(1)}, bf16[256,640]{1,0:T(8,128)(2,1)S(1)}, u32[]{:S(2)}, u32[]{:S(2)}) collective-permute-start(bf16[256,640]{1,0:T(8,128)(2,1)S(1)} %get-tuple-element.65), channel_id=1, source_target_pairs={{0,6},{1,7},{2,0},{3,1},{4,2},{5,3},{6,4},{7,5},{8,14},{9,15},{10,... | collective-permute-start | bytes 983048 | tf_op jit(solution)/shard_map/ppermute | solution.py:31
  134.4 2.8 %collective-permute-start.12 = (bf16[256,640]{1,0:T(8,128)(2,1)S(1)}, bf16[256,640]{1,0:T(8,128)(2,1)}, u32[]{:S(2)}, u32[]{:S(2)}) collective-permute-start(bf16[256,640]{1,0:T(8,128)(2,1)S(1)} %fusion.3), channel_id=1, source_target_pairs={{0,1},{1,0},{2,3},{3,2},{4,5},{5,4},{6,7},{7,6},{8,9},{9,8},{10,11... | collective-permute-start | bytes 983048 | tf_op jit(solution)/shard_map/ppermute | solution.py:31
  137.3 2.9 %collective-permute-start.26 = (bf16[128,16,256]{2,1,0:T(8,128)(2,1)}, bf16[128,16,256]{2,1,0:T(8,128)(2,1)}, u32[]{:S(2)}, u32[]{:S(2)}) collective-permute-start(bf16[128,16,256]{2,1,0:T(8,128)(2,1)} %pad_maximum_fusion.2), channel_id=1, source_target_pairs={{0,8},{8,0},{16,24},{24,16},{32,40},{40,32},{48,56},{56,48},{64,72... | collective-permute-start | bytes 3145736 | tf_op jit(solution)/shard_map/ppermute | solution.py:41
  148.1 7.7 %collective-permute-done.19 = bf16[256,640]{1,0:T(8,128)(2,1)S(1)} collective-permute-done((bf16[256,640]{1,0:T(8,128)(2,1)}, bf16[256,640]{1,0:T(8,128)(2,1)S(1)}, u32[]{:S(2)}, u32[]{:S(2)}) %collective-permute-start.19) | collective-permute-done | bytes 327712 | tf_op jit(solution)/shard_map/ppermute | solution.py:31
  158.1 4.2 %place_pieces.3.refs_3_ = bf16[1024,16,256]{2,1,0:T(8,128)(2,1)} custom-call(s32[8]{0:T(128)} %stack.119.places_ref, bf16[128,16,256]{2,1,0:T(8,128)(2,1)} %get-tuple-element.58.refs_0_, bf16[128,16,256]{2,1,0:T(8,128)(2,1)} %collective-permute-done.14.refs_1_, bf16[128,16,256]{2,1,0:T(8,128)(2,1)} %copy-done.8, ...), custom_call_target="tpu_custom_call" | custom-call | bytes 16777216 | tf_op jit(solution)/shard_map/place_pieces/pallas_call | solution.py:307
  162.4 3.1 %place_pieces.4.refs_3_ = bf16[1024,16,256]{2,1,0:T(8,128)(2,1)} custom-call(s32[4]{0:T(128)} %pad_add_fusion.1.places_ref, bf16[128,16,256]{2,1,0:T(8,128)(2,1)} %get-tuple-element.55.refs_0_, bf16[128,16,256]{2,1,0:T(8,128)(2,1)} %copy-done.10, bf16[128,16,256]{2,1,0:T(8,128)(2,1)} %collective-permute-done.26.refs_2_, ...), custom_call_target="tpu_custom_call", output_to_operand_aliasing={{}: (4, {})} | custom-call | bytes 16777216 | tf_op jit(solution)/shard_map/place_pieces/pallas_call | solution.py:307
  166.5 3.1 %place_pieces.5 = bf16[1024,16,256]{2,1,0:T(8,128)(2,1)} custom-call(s32[4]{0:T(128)} %pad_add_fusion.places_ref, bf16[128,16,256]{2,1,0:T(8,128)(2,1)} %copy-done.11, bf16[128,16,256]{2,1,0:T(8,128)(2,1)} %collective-permute-done.24.refs_1_, bf16[128,16,256]{2,1,0:T(8,128)(2,1)} %copy-done.14, ...), custom_call_target="tpu_custom_call", output_to_operand_aliasing={{}: (4, {})} | custom-call | bytes 16777216 | tf_op jit(solution)/shard_map/place_pieces/pallas_call | solution.py:307
  (122 shorter events, 42.2 us)
Async XLA Ops:
  0.6 19.6 %collective-permute-start = (bf16[4,128,640]{2,1,0:T(8,128)(2,1)}, bf16[4,128,640]{2,1,0:T(8,128)(2,1)S(1)}, u32[]{:S(2)}, u32[]{:S(2)}) collective-permute-start(bf16[4,128,640]{2,1,0:T(8,128)(2,1)} %x0.2), channel_id=1, source_target_pairs={{0,1},{1,0},{2,3},{3,2},{4,5},{5,4},{6,7},{7,6},{8,9},{9,8},{10,11... | collective-permute-start | bytes 1966088 | tf_op jit(solution)/shard_map/ppermute | solution.py:31
  5.1 20.6 %collective-permute-start.3 = (bf16[4,128,640]{2,1,0:T(8,128)(2,1)}, bf16[4,128,640]{2,1,0:T(8,128)(2,1)S(1)}, u32[]{:S(2)}, u32[]{:S(2)}) collective-permute-start(bf16[4,128,640]{2,1,0:T(8,128)(2,1)} %x0.2), channel_id=1, source_target_pairs={{0,2},{1,3},{2,4},{3,5},{4,6},{5,7},{6,0},{7,1},{8,10},{9,11},{10,... | collective-permute-start | bytes 1966088 | tf_op jit(solution)/shard_map/ppermute | solution.py:31
  6.4 19.3 %collective-permute-start.2 = (bf16[4,128,640]{2,1,0:T(8,128)(2,1)}, bf16[4,128,640]{2,1,0:T(8,128)(2,1)S(1)}, u32[]{:S(2)}, u32[]{:S(2)}) collective-permute-start(bf16[4,128,640]{2,1,0:T(8,128)(2,1)} %x0.2), channel_id=1, source_target_pairs={{0,6},{1,7},{2,0},{3,1},{4,2},{5,3},{6,4},{7,5},{8,14},{9,15},{10,... | collective-permute-start | bytes 1966088 | tf_op jit(solution)/shard_map/ppermute | solution.py:31
  7.9 12.4 %collective-permute-start.1 = (s32[256]{0:T(256)}, s32[256]{0:T(256)S(1)}, u32[]{:S(2)}, u32[]{:S(2)}) collective-permute-start(s32[256]{0:T(256)} %bitcast.59), channel_id=1, source_target_pairs={{0,64},{8,72},{16,80},{24,88},{32,96},{40,104},{48,112},{56,120},{... | collective-permute-start | bytes 3080 | tf_op jit(solution)/shard_map/ppermute | solution.py:41
  20.2 15.7 %collective-permute-start.5 = (bf16[4,128,640]{2,1,0:T(8,128)(2,1)S(1)}, bf16[4,128,640]{2,1,0:T(8,128)(2,1)S(1)}, u32[]{:S(2)}, u32[]{:S(2)}) collective-permute-start(bf16[4,128,640]{2,1,0:T(8,128)(2,1)S(1)} %collective-permute-done.x1), channel_id=1, source_target_pairs={{0,6},{1,7},{2,0},{3,1},{4,2},{5,3},{6,4},{7,5},{8,14},{9,15},{10,... | collective-permute-start | bytes 1966088 | tf_op jit(solution)/shard_map/ppermute | solution.py:31
  23.0 24.5 %collective-permute-start.13 = (bf16[128,16,256]{2,1,0:T(8,128)(2,1)}, bf16[128,16,256]{2,1,0:T(8,128)(2,1)S(1)}, u32[]{:S(2)}, u32[]{:S(2)}) collective-permute-start(bf16[128,16,256]{2,1,0:T(8,128)(2,1)} %get-tuple-element.40), channel_id=1, source_target_pairs={{0,32},{8,40},{16,48},{24,56},{32,0},{40,8},{48,16},{56,24},{64,96... | collective-permute-start | bytes 3145736 | tf_op jit(solution)/shard_map/ppermute | solution.py:41
  25.7 54.4 %collective-permute-start.16 = (bf16[256,16,256]{2,1,0:T(8,128)(2,1)}, bf16[256,16,256]{2,1,0:T(8,128)(2,1)}, u32[]{:S(2)}, u32[]{:S(2)}) collective-permute-start(bf16[256,16,256]{2,1,0:T(8,128)(2,1)} %get-tuple-element.37), channel_id=1, source_target_pairs={{0,64},{8,72},{16,80},{24,88},{32,96},{40,104},{48,112},{56,120},{... | collective-permute-start | bytes 6291464 | tf_op jit(solution)/shard_map/ppermute | solution.py:41
  26.5 29.1 %collective-permute-start.6 = (bf16[4,128,640]{2,1,0:T(8,128)(2,1)S(1)}, bf16[4,128,640]{2,1,0:T(8,128)(2,1)S(1)}, u32[]{:S(2)}, u32[]{:S(2)}) collective-permute-start(bf16[4,128,640]{2,1,0:T(8,128)(2,1)S(1)} %collective-permute-done.x1), channel_id=1, source_target_pairs={{0,2},{1,3},{2,4},{3,5},{4,6},{5,7},{6,0},{7,1},{8,10},{9,11},{10,... | collective-permute-start | bytes 1966088 | tf_op jit(solution)/shard_map/ppermute | solution.py:31
  26.6 29.1 %collective-permute-start.4 = (bf16[4,128,640]{2,1,0:T(8,128)(2,1)S(1)}, bf16[4,128,640]{2,1,0:T(8,128)(2,1)S(1)}, u32[]{:S(2)}, u32[]{:S(2)}) collective-permute-start(bf16[4,128,640]{2,1,0:T(8,128)(2,1)S(1)} %collective-permute-done.3.x3), channel_id=1, source_target_pairs={{0,2},{1,3},{2,4},{3,5},{4,6},{5,7},{6,0},{7,1},{8,10},{9,11},{10,... | collective-permute-start | bytes 1966088 | tf_op jit(solution)/shard_map/ppermute | solution.py:31
  35.9 19.7 %collective-permute-start.7 = (bf16[4,128,640]{2,1,0:T(8,128)(2,1)S(1)}, bf16[4,128,640]{2,1,0:T(8,128)(2,1)S(1)}, u32[]{:S(2)}, u32[]{:S(2)}) collective-permute-start(bf16[4,128,640]{2,1,0:T(8,128)(2,1)S(1)} %collective-permute-done.5.x5), channel_id=1, source_target_pairs={{0,6},{1,7},{2,0},{3,1},{4,2},{5,3},{6,4},{7,5},{8,14},{9,15},{10,... | collective-permute-start | bytes 1966088 | tf_op jit(solution)/shard_map/ppermute | solution.py:31
  57.3 22.9 %collective-permute-start.14 = (bf16[128,16,256]{2,1,0:T(8,128)(2,1)}, bf16[128,16,256]{2,1,0:T(8,128)(2,1)}, u32[]{:S(2)}, u32[]{:S(2)}) collective-permute-start(bf16[128,16,256]{2,1,0:T(8,128)(2,1)} %get-tuple-element.41), channel_id=1, source_target_pairs={{0,16},{8,24},{16,32},{24,40},{32,48},{40,56},{48,0},{56,8},{64,80... | collective-permute-start | bytes 3145736 | tf_op jit(solution)/shard_map/ppermute | solution.py:41
  57.6 22.6 %collective-permute-start.15 = (bf16[128,16,256]{2,1,0:T(8,128)(2,1)}, bf16[128,16,256]{2,1,0:T(8,128)(2,1)}, u32[]{:S(2)}, u32[]{:S(2)}) collective-permute-start(bf16[128,16,256]{2,1,0:T(8,128)(2,1)} %get-tuple-element.43), channel_id=1, source_target_pairs={{0,48},{8,56},{16,0},{24,8},{32,16},{40,24},{48,32},{56,40},{64,11... | collective-permute-start | bytes 3145736 | tf_op jit(solution)/shard_map/ppermute | solution.py:41
  85.3 22.2 %collective-permute-start.22 = (bf16[128,16,256]{2,1,0:T(8,128)(2,1)}, bf16[128,16,256]{2,1,0:T(8,128)(2,1)S(1)}, u32[]{:S(2)}, u32[]{:S(2)}) collective-permute-start(bf16[128,16,256]{2,1,0:T(8,128)(2,1)} %get-tuple-element.51), channel_id=1, source_target_pairs={{0,32},{8,40},{16,48},{24,56},{32,0},{40,8},{48,16},{56,24},{64,96... | collective-permute-start | bytes 3145736 | tf_op jit(solution)/shard_map/ppermute | solution.py:41
  86.6 22.4 %collective-permute-start.8 = (bf16[2,256,640]{2,1,0:T(8,128)(2,1)}, bf16[2,256,640]{2,1,0:T(8,128)(2,1)}, u32[]{:S(2)}, u32[]{:S(2)}) collective-permute-start(bf16[2,256,640]{2,1,0:T(8,128)(2,1)} %get-tuple-element.35), channel_id=1, source_target_pairs={{0,6},{1,7},{2,0},{3,1},{4,2},{5,3},{6,4},{7,5},{8,14},{9,15},{10,... | collective-permute-start | bytes 1966088 | tf_op jit(solution)/shard_map/ppermute | solution.py:31
  86.6 25.2 %collective-permute-start.9 = (bf16[2,256,640]{2,1,0:T(8,128)(2,1)}, bf16[2,256,640]{2,1,0:T(8,128)(2,1)}, u32[]{:S(2)}, u32[]{:S(2)}) collective-permute-start(bf16[2,256,640]{2,1,0:T(8,128)(2,1)} %get-tuple-element.36), channel_id=1, source_target_pairs={{0,2},{1,3},{2,4},{3,5},{4,6},{5,7},{6,0},{7,1},{8,10},{9,11},{10,... | collective-permute-start | bytes 1966088 | tf_op jit(solution)/shard_map/ppermute | solution.py:31
  103.3 16.4 %collective-permute-start.17 = (bf16[2,256,640]{2,1,0:T(8,128)(2,1)}, bf16[2,256,640]{2,1,0:T(8,128)(2,1)}, u32[]{:S(2)}, u32[]{:S(2)}) collective-permute-start(bf16[2,256,640]{2,1,0:T(8,128)(2,1)} %get-tuple-element.48), channel_id=1, source_target_pairs={{0,6},{1,7},{2,0},{3,1},{4,2},{5,3},{6,4},{7,5},{8,14},{9,15},{10,... | collective-permute-start | bytes 1966088 | tf_op jit(solution)/shard_map/ppermute | solution.py:31
  104.6 17.3 %collective-permute-start.18 = (bf16[2,256,640]{2,1,0:T(8,128)(2,1)}, bf16[2,256,640]{2,1,0:T(8,128)(2,1)}, u32[]{:S(2)}, u32[]{:S(2)}) collective-permute-start(bf16[2,256,640]{2,1,0:T(8,128)(2,1)} %get-tuple-element.49), channel_id=1, source_target_pairs={{0,2},{1,3},{2,4},{3,5},{4,6},{5,7},{6,0},{7,1},{8,10},{9,11},{10,... | collective-permute-start | bytes 1966088 | tf_op jit(solution)/shard_map/ppermute | solution.py:31
  107.5 26.9 %collective-permute-start.23 = (bf16[128,16,256]{2,1,0:T(8,128)(2,1)}, bf16[128,16,256]{2,1,0:T(8,128)(2,1)S(1)}, u32[]{:S(2)}, u32[]{:S(2)}) collective-permute-start(bf16[128,16,256]{2,1,0:T(8,128)(2,1)} %get-tuple-element.52), channel_id=1, source_target_pairs={{0,16},{8,24},{16,32},{24,40},{32,48},{40,56},{48,0},{56,8},{64,80... | collective-permute-start | bytes 3145736 | tf_op jit(solution)/shard_map/ppermute | solution.py:41
  109.0 28.3 %collective-permute-start.24 = (bf16[128,16,256]{2,1,0:T(8,128)(2,1)}, bf16[128,16,256]{2,1,0:T(8,128)(2,1)}, u32[]{:S(2)}, u32[]{:S(2)}) collective-permute-start(bf16[128,16,256]{2,1,0:T(8,128)(2,1)} %get-tuple-element.54), channel_id=1, source_target_pairs={{0,48},{8,56},{16,0},{24,8},{32,16},{40,24},{48,32},{56,40},{64,11... | collective-permute-start | bytes 3145736 | tf_op jit(solution)/shard_map/ppermute | solution.py:41
  111.8 46.3 %collective-permute-start.27 = (bf16[256,16,256]{2,1,0:T(8,128)(2,1)}, bf16[256,16,256]{2,1,0:T(8,128)(2,1)}, u32[]{:S(2)}, u32[]{:S(2)}) collective-permute-start(bf16[256,16,256]{2,1,0:T(8,128)(2,1)} %pad_maximum_fusion), channel_id=1, source_target_pairs={{0,8},{8,0},{16,24},{24,16},{32,40},{40,32},{48,56},{56,48},{64,72... | collective-permute-start | bytes 6291464 | tf_op jit(solution)/shard_map/ppermute | solution.py:41
  121.9 23.7 %collective-permute-start.10 = (bf16[256,640]{1,0:T(8,128)(2,1)}, bf16[256,640]{1,0:T(8,128)(2,1)}, u32[]{:S(2)}, u32[]{:S(2)}) collective-permute-start(bf16[256,640]{1,0:T(8,128)(2,1)} %get-tuple-element.62), channel_id=1, source_target_pairs={{0,2},{1,3},{2,4},{3,5},{4,6},{5,7},{6,0},{7,1},{8,10},{9,11},{10,... | collective-permute-start | bytes 983048 | tf_op jit(solution)/shard_map/ppermute | solution.py:31
  128.9 13.4 %collective-permute-start.20 = (bf16[256,640]{1,0:T(8,128)(2,1)S(1)}, bf16[256,640]{1,0:T(8,128)(2,1)S(1)}, u32[]{:S(2)}, u32[]{:S(2)}) collective-permute-start(bf16[256,640]{1,0:T(8,128)(2,1)S(1)} %get-tuple-element.65), channel_id=1, source_target_pairs={{0,6},{1,7},{2,0},{3,1},{4,2},{5,3},{6,4},{7,5},{8,14},{9,15},{10,... | collective-permute-start | bytes 983048 | tf_op jit(solution)/shard_map/ppermute | solution.py:31
  137.3 25.1 %collective-permute-start.26 = (bf16[128,16,256]{2,1,0:T(8,128)(2,1)}, bf16[128,16,256]{2,1,0:T(8,128)(2,1)}, u32[]{:S(2)}, u32[]{:S(2)}) collective-permute-start(bf16[128,16,256]{2,1,0:T(8,128)(2,1)} %pad_maximum_fusion.2), channel_id=1, source_target_pairs={{0,8},{8,0},{16,24},{24,16},{32,40},{40,32},{48,56},{56,48},{64,72... | collective-permute-start | bytes 3145736 | tf_op jit(solution)/shard_map/ppermute | solution.py:41
  143.1 22.4 %collective-permute-start.25 = (bf16[128,16,256]{2,1,0:T(8,128)(2,1)}, bf16[128,16,256]{2,1,0:T(8,128)(2,1)S(1)}, u32[]{:S(2)}, u32[]{:S(2)}) collective-permute-start(bf16[128,16,256]{2,1,0:T(8,128)(2,1)} %pad_maximum_fusion.1), channel_id=1, source_target_pairs={{0,8},{8,0},{16,24},{24,16},{32,40},{40,32},{48,56},{56,48},{64,72... | collective-permute-start | bytes 3145736 | tf_op jit(solution)/shard_map/ppermute | solution.py:41
  (25 other events, 448.7 us)

commit v3 on v2

--- a/solution.py
+++ b/solution.py
@@ -23,7 +23,7 @@
 def places(relative):
     me = lax.axis_index("tp")
     y, z = me // 2, me % 2
-    return jnp.stack([((y + dy) % 4) * 2 + (z + dz) % 2 for dy, dz in relative]).astype(jnp.int32)
+    return [((y + dy) % 4) * 2 + (z + dz) % 2 for dy, dz in relative]
 
 
 def tp_move(array, dy, dz):
@@ -42,8 +42,8 @@
 
 
 def decode_kernel(
-    rows, first_row, where, table, x0, x1, x2, x3, x4, x5, x6, x7, gain, wq, wk, wv, wo, pool,
-    lane_row, query_gain, key_gain, plus, minus, local,
+    rows, first_row, table, lengths, x0, x1, x2, x3, x4, x5, x6, x7, gain, wq, wk, wv, wo, pool,
+    query_gain, key_gain, plus, minus, local,
     x_v, wq_v, wk_v, wv_v, wo_v, pool_v, qkv, ctx, out_v, sems,
 ):
     steps = 4
@@ -51,6 +51,7 @@
     width = x0.shape[2]
     count = steps * rows
     xs = (x0, x1, x2, x3, x4, x5, x6, x7)
+    where = places(GATHERED + SCATTERED)
     w_copies, o_copies = [], []
     for k in range(8):
         span = pl.ds(pl.multiple_of(where[k] * width, width), width)
@@ -112,6 +113,8 @@
     query_step = lax.broadcasted_iota(jnp.int32, (height, 1), 0) // (groups * GROUP)
     fresh_lane = lax.broadcasted_iota(jnp.int32, (1, steps * GROUP), 1)
     fresh_ok = (fresh_lane % GROUP == query_row) & (fresh_lane // GROUP <= query_step)
+    lane = lax.broadcasted_iota(jnp.int32, (1, GROUP * 6 * PAGE), 1)
+    lane_row, lane_place = lane // (6 * PAGE), lane % (6 * PAGE)
     scale = HEAD ** (-0.5)
     contract_last = (((1,), (1,)), ((), ()))
 
@@ -130,12 +133,16 @@
         ).astype(jnp.bfloat16)
         fresh_k = jnp.concatenate(tiles(4), axis=0).astype(jnp.bfloat16)
         fresh_v = jnp.concatenate(tiles(5), axis=0).astype(jnp.bfloat16)
-        blocks = [pool_v[table[first_row * 6 + i * (GROUP * 6) + j]] for j in range(GROUP * 6)]
+        blocks = [pool_v[table[j % 6, first_row + i * GROUP + j // 6]] for j in range(GROUP * 6)]
         cached_k = jnp.concatenate([b[:, :HEAD] for b in blocks], axis=0)
         cached_v = jnp.concatenate([b[:, HEAD:] for b in blocks], axis=0)
         scores = lax.dot_general(queries, cached_k, contract_last, preferred_element_type=jnp.float32)
         fresh = lax.dot_general(queries, fresh_k, contract_last, preferred_element_type=jnp.float32)
-        scores = jnp.where(lane_row[first_row // GROUP + i] == query_row, scores * scale, NEG)
+        used = jnp.full(lane.shape, -1, jnp.int32)
+        for r in range(GROUP):
+            length = lengths[first_row + i * GROUP + r]
+            used = jnp.where((lane_row == r) & (lane_place < length), r, used)
+        scores = jnp.where(used == query_row, scores * scale, NEG)
         fresh = jnp.where(fresh_ok, fresh * scale, NEG)
         top = jnp.maximum(
             jnp.max(scores, axis=1, keepdims=True), jnp.max(fresh, axis=1, keepdims=True)
@@ -174,7 +181,7 @@
 
 
 def decode(
-    rows, first_row, where, table, xs, gain, wq, wk, wv, wo, pool, lane_row, query_gain, key_gain
+    rows, first_row, table, lengths, xs, gain, wq, wk, wv, wo, pool, query_gain, key_gain
 ):
     steps, _, width = xs[0].shape
     count = steps * rows
@@ -189,7 +196,7 @@
             jax.ShapeDtypeStruct((2, count, width), bf16),
             jax.ShapeDtypeStruct((4, count, width), bf16),
         ),
-        in_specs=[smem] * 2 + [hbm] * 8 + [vmem] + [hbm] * 5 + [vmem] * 3,
+        in_specs=[smem] * 2 + [hbm] * 8 + [vmem] + [hbm] * 5 + [vmem] * 2,
         out_specs=(hbm, hbm, hbm),
         scratch_shapes=[
             pltpu.VMEM((8, steps, rows, width), bf16),
@@ -208,7 +215,7 @@
             flops=2 * count * 5120 * 1280, bytes_accessed=24 * MIB, transcendentals=0
         ),
         name="decode_rows",
-    )(where, table, *xs, gain, wq, wk, wv, wo, pool, lane_row, query_gain, key_gain)
+    )(table, lengths, *xs, gain, wq, wk, wv, wo, pool, query_gain, key_gain)
 
 
 def slots_kernel(table, order, blocks, *refs):
@@ -254,7 +261,7 @@
         out_specs=(hbm,) * len(heights),
         scratch_shapes=[pltpu.VMEM((2 * CAP,) + tail, blocks.dtype)] * 4
         + [
-            pltpu.VMEM((order.shape[0],) + tail, blocks.dtype),
+            pltpu.VMEM((order.shape[0] if with_compact else 8,) + tail, blocks.dtype),
             pltpu.VMEM((blocks.shape[0] + 1,) + tail, blocks.dtype),
             pltpu.SemaphoreType.DMA((6,)),
         ],
@@ -276,7 +283,9 @@
 
 
 def cross(received):
-    return inst_move(jnp.concatenate([r[CAP:] for r in received]), 0, 0, 1)
+    offsets = [(j, 1) for j in range(len(received))]
+    order = jnp.arange(len(received), dtype=jnp.int32)
+    return inst_move(place_pieces(order, received, offsets, None, len(received)), 0, 0, 1)
 
 
 def place_kernel(offsets, places_ref, *refs):
@@ -297,12 +306,12 @@
         copy.wait()
 
 
-def place_pieces(where, arrays, offsets, before):
+def place_pieces(where, arrays, offsets, before, count=16):
     smem = pl.BlockSpec(memory_space=pltpu.SMEM)
     either = pl.BlockSpec(memory_space=pl.ANY)
     hbm = pl.BlockSpec(memory_space=pltpu.HBM)
     blocks = arrays[0].shape[1:]
-    shape = jax.ShapeDtypeStruct((16 * CAP,) + blocks, arrays[0].dtype)
+    shape = jax.ShapeDtypeStruct((count * CAP,) + blocks, arrays[0].dtype)
     extra = [] if before is None else [before]
     return pl.pallas_call(
         functools.partial(place_kernel, tuple(offsets)),
@@ -342,14 +351,20 @@
     return below, above, up, down
 
 
-def scatter_rest(local, below, above, up, down):
-    f32, bf16 = jnp.float32, jnp.bfloat16
-    from_below = tp_move(up, 1, 0)
-    from_above = tp_move(down, 3, 0)
-    other = (local[3].astype(f32) + below[1].astype(f32) + from_above.astype(f32)).astype(bf16)
-    crossed = tp_move(other, 0, 1)
+def scatter_second(up, down):
+    return tp_move(up, 1, 0), tp_move(down, 3, 0)
+
+
+def scatter_third(local, below, from_above):
+    f32 = jnp.float32
+    total = local[3].astype(f32) + below[1].astype(f32) + from_above.astype(f32)
+    return total.astype(jnp.bfloat16)
+
+
+def scatter_last(local, above, from_below, crossed):
+    f32 = jnp.float32
     mine = local[2].astype(f32) + above[1].astype(f32) + from_below.astype(f32)
-    return (mine + crossed.astype(f32)).astype(bf16)
+    return (mine + crossed.astype(f32)).astype(jnp.bfloat16)
 
 
 def body(
@@ -389,16 +404,9 @@
     other_table = slot_table(other_target, order, order.shape[0], own_z, own_x, own_c)
 
     gain = norm_gain.reshape(8, 1, width)
-    positions = jnp.arange(block_table.shape[1] * PAGE, dtype=jnp.int32)
-    lane_row = jnp.where(
-        positions[None, :] < cache_len[:, None],
-        (jnp.arange(row_count, dtype=jnp.int32) % GROUP)[:, None],
-        -1,
-    ).reshape(row_count // GROUP, 1, -1)
-    tp_where = places(GATHERED + SCATTERED)
     query_gain = query_gain.reshape(1, HEAD)
     key_gain = key_gain.reshape(1, HEAD)
-    blocks_of_rows = block_table.reshape(-1)
+    blocks_of_rows = block_table.T
     def where(z):
         return jnp.stack(
             [z * 8 + ((own_x - j % 4) % 4) * 2 + (own_c + j // 4) % 2 for j in range(8)]
@@ -407,41 +415,46 @@
 
     def decode_part(c):
         return decode(
-            rows, c * rows, tp_where, blocks_of_rows, gathered, gain, query_weight, key_weight,
-            value_weight, output_weight, kv_pool, lane_row, query_gain, key_gain,
+            rows, c * rows, blocks_of_rows, cache_len, gathered, gain, query_weight, key_weight,
+            value_weight, output_weight, kv_pool, query_gain, key_gain,
         )
 
     plus, minus, local = decode_part(0)
     sums = scatter_first(plus, minus, local)
     other_table = after(other_table, near, back, plus)
-    other_slots = fill_slots(other_table, order, other_blocks, False)
+    other_slots = fill_slots(other_table, other_table, other_blocks, False)
     other_far = inst_move(other_slots[2], 0, 2, 0)
-    gathered[0] = after(gathered[0], other_slots[0])
+    gathered[0] = after(gathered[0], other_slots[0], *sums[2:])
+    seconds = scatter_second(*sums[2:])
     later_parts = decode_part(1)
-    later_sums = scatter_first(*later_parts)
-    chunks = [scatter_rest(local, *sums), scatter_rest(later_parts[2], *later_sums)]
+    later_sums = scatter_first(
+        after(later_parts[0], *seconds), after(later_parts[1], *seconds), later_parts[2]
+    )
+    later_seconds = scatter_second(*later_sums[2:])
+    other_near = inst_move(after(other_slots[1], other_far, later_parts[0]), 0, 1, 0)
+    other_back = inst_move(after(other_slots[3], other_far, later_parts[0]), 0, 3, 0)
+
+    def where(z):
+        return jnp.stack(
+            [z * 8 + ((own_x - dx) % 4) * 2 + (own_c + dc) % 2 for dc in (0, 1) for dx in range(4)]
+        ).astype(jnp.int32)
+
+    offsets = [(j, 0) for j in range(4)] + [(4, j) for j in range(4)]
+    pieces = [slots[0], near, far, back]
+    pieces.append(cross(after(pieces, *seconds)))
+    arrived = place_pieces(where(own_z), pieces, offsets, None)
+    other = scatter_third(local, sums[0], seconds[1])
+    chunks = [scatter_last(local, sums[1], seconds[0], tp_move(other, 0, 1))]
+    later = scatter_third(later_parts[2], later_sums[0], after(later_seconds[1], later_seconds[0]))
+    later_crossed = after(tp_move(later, 0, 1), arrived)
+    chunks.append(scatter_last(later_parts[2], later_sums[1], later_seconds[0], later_crossed))
     mixed_out = jnp.concatenate(
         [chunk.reshape(step_count, rows, width) for chunk in chunks], axis=1
     )
-
-    def where(z, far_xs, cores):
-        return jnp.stack(
-            [z * 8 + ((own_x - dx) % 4) * 2 + (own_c + dc) % 2 for dc in cores for dx in far_xs]
-        ).astype(jnp.int32)
-
-    other_near = inst_move(after(other_slots[1], other_far, later_parts[0]), 0, 1, 0)
-    other_back = inst_move(after(other_slots[3], other_far, later_parts[0]), 0, 3, 0)
-    pieces = [slots[0], near, far, back]
-    pieces.append(cross(after(pieces, later_parts[0])))
-    offsets = [(j, 0) for j in range(4)] + [(4, j) for j in range(4)]
-    arrived = place_pieces(where(own_z, (0, 1, 2, 3), (0, 1)), pieces, offsets, None)
-    pieces = [other_slots[0], other_far]
-    pieces.append(cross(after(pieces, later_parts[0])))
-    offsets = [(0, 0), (1, 0), (2, 0), (2, 1)]
-    arrived = place_pieces(where(1 - own_z, (0, 2), (0, 1)), pieces, offsets, arrived)
-    pieces = [other_near, other_back]
-    pieces.append(cross(pieces))
-    arrived = place_pieces(where(1 - own_z, (1, 3), (0, 1)), pieces, offsets, arrived)
+    pieces = [other_slots[0], other_near, other_far, other_back]
+    pieces.append(cross(after(pieces, later, chunks[0])))
+    pieces[0] = after(pieces[0], mixed_out)
+    arrived = place_pieces(where(1 - own_z), pieces, offsets, arrived)
     return (mixed_out, arrived)
 
 

time: 170 us -> 162 us (0.953)
  other arithmetic: 20 us -> 14 us
  local copies, waits for them, and re-layouts: 11.4 us -> 6.21 us
  Pallas kernels: 52.2 us -> 56.9 us
  waiting for transfers between devices: 40.9 us -> 38.6 us
    pallas_call x3 -> x4, Pallas kernels: 10.4 us -> 14.9 us  [place_pieces(): pl.pallas_call(functools.partial(place_kernel, tuple(offsets)), out_shape...]
    concatenate x3 -> x0, other arithmetic: 3.75 us -> none  [cross(): return inst_move(jnp.concatenate([r[CAP:] for r in received]), 0, 0, 1)]
    slice x9 -> x0, local copies, waits for them, and re-layouts: 3.43 us -> none  [cross(): return inst_move(jnp.concatenate([r[CAP:] for r in received]), 0, 0, 1)]
    convert_element_type x2 -> x1, other arithmetic: 4.24 us -> 1.16 us  [scatter_first(): up = (local[0].astype(f32) + below[0].astype(f32)).astype(bf16)]
    convert_element_type x4 -> x5, other arithmetic: 5.06 us -> 7.86 us  [the longest x2 3.12 us: scatter_third(): return total.astype(jnp.bfloat16)]
    ppermute x17, waiting for transfers between devices: 29.5 us -> 26.7 us  [tp_move(): return lax.ppermute(array, 'tp', pairs)]
    ppermute x17, starting transfers between devices: 24.4 us -> 26.9 us  [tp_move(): return lax.ppermute(array, 'tp', pairs)]
    ppermute x11 -> x10, starting transfers between devices: 19.7 us -> 17.9 us  [inst_move(): return lax.ppermute(array, 'inst', pairs)]
  transfers between devices with their start and end apart: 28 -> 27, of which waited for: 9 -> 9; matrix products, arithmetic and copies ran while one was open for 16% -> 11% of each run, Pallas kernels for 26% -> 33%
where the time goes in v3:
time: 162 us
  Pallas kernels  56.9 us (35%)
  starting transfers between devices  44.9 us (28%)
  waiting for transfers between devices  38.6 us (24%)
  other arithmetic  14 us (9%)
  local copies, waits for them, and re-layouts  6.21 us (4%)
    pallas_call x2, Pallas kernels, decode(): pl.pallas_call(functools.partial(decode_kernel, rows, first_row), out_sha...  30.7 us
    ppermute x17, starting transfers between devices, tp_move(): return lax.ppermute(array, 'tp', pairs)  26.9 us
    ppermute x17, waiting for transfers between devices, tp_move(): return lax.ppermute(array, 'tp', pairs)  26.7 us
    ppermute x10, starting transfers between devices, inst_move(): return lax.ppermute(array, 'inst', pairs)  17.9 us
    pallas_call x4, Pallas kernels, place_pieces(): pl.pallas_call(functools.partial(place_kernel, tuple(offsets)), out_shape...  14.9 us
    ppermute x10, waiting for transfers between devices, inst_move(): return lax.ppermute(array, 'inst', pairs)  11.9 us
    pallas_call x2, Pallas kernels, fill_slots(): pl.pallas_call(slots_kernel, out_shape=tuple((jax.ShapeDtypeStruct((n,) +...  11.3 us
  transfers between devices with their start and end apart: 27, of which 9 were waited for; matrix products, arithmetic and copies ran while one was open for 11% of the time, Pallas kernels for 33%

profile of v3, /device:TPU:1, one launch (start us, length us, event | category | flops | bytes accessed | tf_op | source)
XLA Modules:
  0.0 161.7 jit_solution(15233370614938067689)
XLA Ops:
  0.6 4.5 %collective-permute-start = (bf16[4,128,640]{2,1,0:T(8,128)(2,1)}, bf16[4,128,640]{2,1,0:T(8,128)(2,1)S(1)}, u32[]{:S(2)}, u32[]{:S(2)}) collective-permute-start(bf16[4,128,640]{2,1,0:T(8,128)(2,1)} %x0.2), channel_id=1, source_target_pairs={{0,1},{1,0},{2,3},{3,2},{4,5},{5,4},{6,7},{7,6},{8,9},{9,8},{10,11... | collective-permute-start | bytes 1966088 | tf_op jit(solution)/shard_map/ppermute | solution.py:31
  11.7 6.7 %fill_slots.2 = (bf16[128,16,256]{2,1,0:T(8,128)(2,1)}, bf16[128,16,256]{2,1,0:T(8,128)(2,1)}, bf16[128,16,256]{2,1,0:T(8,128)(2,1)}, bf16[128,16,256]{2,1,0:T(8,128)(2,1)}, bf16[256,16,256]{2,1,0:T(8,128)(2,1)}) custom-call(s32[512]{0:T(512)} %select_reduce_fusion.1.table, s32[256]{0:T(256)} %order.1, bf16[768,16,256]{2,1,0:T(8,128)(2,1)} %pool.3), custom_call_target="tpu_custom_call" | custom-call | bytes 16777216 | tf_op jit(solution)/shard_map/fill_slots/pallas_call | solution.py:257
  20.2 2.7 %collective-permute-start.5 = (bf16[4,128,640]{2,1,0:T(8,128)(2,1)S(1)}, bf16[4,128,640]{2,1,0:T(8,128)(2,1)S(1)}, u32[]{:S(2)}, u32[]{:S(2)}) collective-permute-start(bf16[4,128,640]{2,1,0:T(8,128)(2,1)S(1)} %collective-permute-done.x1), channel_id=1, source_target_pairs={{0,6},{1,7},{2,0},{3,1},{4,2},{5,3},{6,4},{7,5},{8,14},{9,15},{10,... | collective-permute-start | bytes 1966088 | tf_op jit(solution)/shard_map/ppermute | solution.py:31
  23.0 2.7 %collective-permute-start.13 = (bf16[128,16,256]{2,1,0:T(8,128)(2,1)}, bf16[128,16,256]{2,1,0:T(8,128)(2,1)S(1)}, u32[]{:S(2)}, u32[]{:S(2)}) collective-permute-start(bf16[128,16,256]{2,1,0:T(8,128)(2,1)} %get-tuple-element.47), channel_id=1, source_target_pairs={{0,32},{8,40},{16,48},{24,56},{32,0},{40,8},{48,16},{56,24},{64,96... | collective-permute-start | bytes 3145736 | tf_op jit(solution)/shard_map/ppermute | solution.py:41
  26.6 9.3 %collective-permute-done.5.x5 = bf16[4,128,640]{2,1,0:T(8,128)(2,1)S(1)} collective-permute-done((bf16[4,128,640]{2,1,0:T(8,128)(2,1)S(1)}, bf16[4,128,640]{2,1,0:T(8,128)(2,1)S(1)}, u32[]{:S(2)}, u32[]{:S(2)}) %collective-permute-start.5) | collective-permute-done | bytes 655392 | tf_op jit(solution)/shard_map/ppermute | solution.py:31
  35.9 3.0 %collective-permute-start.7 = (bf16[4,128,640]{2,1,0:T(8,128)(2,1)S(1)}, bf16[4,128,640]{2,1,0:T(8,128)(2,1)S(1)}, u32[]{:S(2)}, u32[]{:S(2)}) collective-permute-start(bf16[4,128,640]{2,1,0:T(8,128)(2,1)S(1)} %collective-permute-done.5.x5), channel_id=1, source_target_pairs={{0,6},{1,7},{2,0},{3,1},{4,2},{5,3},{6,4},{7,5},{8,14},{9,15},{10,... | collective-permute-start | bytes 1966088 | tf_op jit(solution)/shard_map/ppermute | solution.py:31
  38.9 8.6 %collective-permute-done.13.refs_2_ = bf16[128,16,256]{2,1,0:T(8,128)(2,1)S(1)} collective-permute-done((bf16[128,16,256]{2,1,0:T(8,128)(2,1)}, bf16[128,16,256]{2,1,0:T(8,128)(2,1)S(1)}, u32[]{:S(2)}, u32[]{:S(2)}) %collective-permute-start.13) | collective-permute-done | bytes 1048608 | tf_op jit(solution)/shard_map/ppermute | solution.py:41
  47.5 8.1 %collective-permute-done.4.x4 = bf16[4,128,640]{2,1,0:T(8,128)(2,1)S(1)} collective-permute-done((bf16[4,128,640]{2,1,0:T(8,128)(2,1)S(1)}, bf16[4,128,640]{2,1,0:T(8,128)(2,1)S(1)}, u32[]{:S(2)}, u32[]{:S(2)}) %collective-permute-start.4) | collective-permute-done | bytes 655392 | tf_op jit(solution)/shard_map/ppermute | solution.py:31
  59.1 15.4 %decode_rows.2 = (bf16[2,256,640]{2,1,0:T(8,128)(2,1)}, bf16[2,256,640]{2,1,0:T(8,128)(2,1)}, bf16[4,256,640]{2,1,0:T(8,128)(2,1)}) custom-call(s32[6,128]{1,0:T(8,128)} %bitcast.52, s32[128]{0:T(128)} %lengths.3, bf16[4,128,640]{2,1,0:T(8,128)(2,1)} %x0.2, bf16[4,128,640]{2,1,0:T(8,128)(2,1)} %copy-done.6, bf16[4,128,640]{2,1,0:T(8,128)(2,1)} %copy-done.8, ...), custom_call_target="tpu_custom_call" | custom-call | flops 3355443200 | bytes 25165824 | tf_op jit(solution)/shard_map/decode_rows/pallas_call | solution.py:192
  78.5 4.6 %fill_slots.3 = (bf16[128,16,256]{2,1,0:T(8,128)(2,1)}, bf16[128,16,256]{2,1,0:T(8,128)(2,1)}, bf16[128,16,256]{2,1,0:T(8,128)(2,1)}, bf16[128,16,256]{2,1,0:T(8,128)(2,1)}) custom-call(s32[512]{0:T(512)} %select_reduce_fusion.table.order, s32[512]{0:T(512)} %select_reduce_fusion.table.order, bf16[256,16,256]{2,1,0:T(8,128)(2,1)} %collective-permute-done.16.blocks), custom_call_target="tpu_custom_call" | custom-call | bytes 16777216 | tf_op jit(solution)/shard_map/fill_slots/pallas_call | solution.py:257
  84.5 2.8 %collective-permute-done.8 = bf16[2,256,640]{2,1,0:T(8,128)(2,1)} collective-permute-done((bf16[2,256,640]{2,1,0:T(8,128)(2,1)}, bf16[2,256,640]{2,1,0:T(8,128)(2,1)}, u32[]{:S(2)}, u32[]{:S(2)}) %collective-permute-start.8) | collective-permute-done | bytes 655392 | tf_op jit(solution)/shard_map/ppermute | solution.py:31
  88.8 2.2 %fusion.7 = (bf16[256,640]{1,0:T(8,128)(2,1)}, bf16[256,640]{1,0:T(8,128)(2,1)S(1)}) fusion(bf16[2,256,640]{2,1,0:T(8,128)(2,1)} %collective-permute-done.8, bf16[4,256,640]{2,1,0:T(8,128)(2,1)} %get-tuple-element.41, bf16[2,256,640]{2,1,0:T(8,128)(2,1)} %collective-permute-done.9), kind=kLoop, calls=%fused_computation.18 | loop fusion | flops 1310720 | bytes 1966080 | tf_op jit(solution)/shard_map/convert_element_type | solution.py:350
  92.4 15.3 %decode_rows.3 = (bf16[2,256,640]{2,1,0:T(8,128)(2,1)}, bf16[2,256,640]{2,1,0:T(8,128)(2,1)}, bf16[4,256,640]{2,1,0:T(8,128)(2,1)}) custom-call(s32[6,128]{1,0:T(8,128)} %bitcast.53, s32[128]{0:T(128)} %lengths.3, bf16[4,128,640]{2,1,0:T(8,128)(2,1)} %x0.2, bf16[4,128,640]{2,1,0:T(8,128)(2,1)} %copy-done.6, bf16[4,128,640]{2,1,0:T(8,128)(2,1)} %copy-done.8, ...), custom_call_target="tpu_custom_call" | custom-call | flops 3355443200 | bytes 25165824 | tf_op jit(solution)/shard_map/decode_rows/pallas_call | solution.py:192
  107.9 2.7 %collective-permute-start.17 = (bf16[2,256,640]{2,1,0:T(8,128)(2,1)}, bf16[2,256,640]{2,1,0:T(8,128)(2,1)S(1)}, u32[]{:S(2)}, u32[]{:S(2)}) collective-permute-start(bf16[2,256,640]{2,1,0:T(8,128)(2,1)} %get-tuple-element.56), channel_id=1, source_target_pairs={{0,6},{1,7},{2,0},{3,1},{4,2},{5,3},{6,4},{7,5},{8,14},{9,15},{10,... | collective-permute-start | bytes 1966088 | tf_op jit(solution)/shard_map/ppermute | solution.py:31
  110.7 2.6 %collective-permute-start.25 = (bf16[128,16,256]{2,1,0:T(8,128)(2,1)}, bf16[128,16,256]{2,1,0:T(8,128)(2,1)S(1)}, u32[]{:S(2)}, u32[]{:S(2)}) collective-permute-start(bf16[128,16,256]{2,1,0:T(8,128)(2,1)} %get-tuple-element.71), channel_id=1, source_target_pairs={{0,48},{8,56},{16,0},{24,8},{32,16},{40,24},{48,32},{56,40},{64,11... | collective-permute-start | bytes 3145736 | tf_op jit(solution)/shard_map/ppermute | solution.py:41
  114.5 2.9 %collective-permute-start.12 = (bf16[256,640]{1,0:T(8,128)(2,1)S(1)}, bf16[256,640]{1,0:T(8,128)(2,1)}, u32[]{:S(2)}, u32[]{:S(2)}) collective-permute-start(bf16[256,640]{1,0:T(8,128)(2,1)S(1)} %fusion.3), channel_id=1, source_target_pairs={{0,1},{1,0},{2,3},{3,2},{4,5},{5,4},{6,7},{7,6},{8,9},{9,8},{10,11... | collective-permute-start | bytes 983048 | tf_op jit(solution)/shard_map/ppermute | solution.py:31
  117.4 2.8 %collective-permute-done.18 = bf16[2,256,640]{2,1,0:T(8,128)(2,1)S(1)} collective-permute-done((bf16[2,256,640]{2,1,0:T(8,128)(2,1)}, bf16[2,256,640]{2,1,0:T(8,128)(2,1)S(1)}, u32[]{:S(2)}, u32[]{:S(2)}) %collective-permute-start.18) | collective-permute-done | bytes 655392 | tf_op jit(solution)/shard_map/ppermute | solution.py:31
  121.5 2.5 %collective-permute-start.20 = (bf16[256,640]{1,0:T(8,128)(2,1)}, bf16[256,640]{1,0:T(8,128)(2,1)S(1)}, u32[]{:S(2)}, u32[]{:S(2)}) collective-permute-start(bf16[256,640]{1,0:T(8,128)(2,1)} %get-tuple-element.77), channel_id=1, source_target_pairs={{0,6},{1,7},{2,0},{3,1},{4,2},{5,3},{6,4},{7,5},{8,14},{9,15},{10,... | collective-permute-start | bytes 983048 | tf_op jit(solution)/shard_map/ppermute | solution.py:31
  124.6 3.2 %place_pieces.4 = bf16[256,16,256]{2,1,0:T(8,128)(2,1)} custom-call(s32[4]{0:T(128)} %iota.28.places_ref, bf16[128,16,256]{2,1,0:T(8,128)(2,1)} %get-tuple-element.61.refs_0_, bf16[128,16,256]{2,1,0:T(8,128)(2,1)} %copy-done.1, bf16[128,16,256]{2,1,0:T(8,128)(2,1)} %copy-done, bf16[128,16,256]{2,1,0:T(8,128)(2,1)} %copy-done.2), custom_call_target="tpu_custom_call" | custom-call | bytes 16777216 | tf_op jit(solution)/shard_map/place_pieces/pallas_call | solution.py:316
  127.8 7.4 %collective-permute-start.22 = (bf16[256,16,256]{2,1,0:T(8,128)(2,1)}, bf16[256,16,256]{2,1,0:T(8,128)(2,1)}, u32[]{:S(2)}, u32[]{:S(2)}) collective-permute-start(bf16[256,16,256]{2,1,0:T(8,128)(2,1)} %place_pieces.4), channel_id=1, source_target_pairs={{0,8},{8,0},{16,24},{24,16},{32,40},{40,32},{48,56},{56,48},{64,72... | collective-permute-start | bytes 6291464 | tf_op jit(solution)/shard_map/ppermute | solution.py:41
  139.9 3.1 %place_pieces.6 = bf16[256,16,256]{2,1,0:T(8,128)(2,1)} custom-call(s32[4]{0:T(128)} %iota.29.places_ref, bf16[128,16,256]{2,1,0:T(8,128)(2,1)} %get-tuple-element.72.refs_0_, bf16[128,16,256]{2,1,0:T(8,128)(2,1)} %copy-done.4, bf16[128,16,256]{2,1,0:T(8,128)(2,1)} %copy-done.3, bf16[128,16,256]{2,1,0:T(8,128)(2,1)} %copy-done.5), custom_call_target="tpu_custom_call" | custom-call | bytes 16777216 | tf_op jit(solution)/shard_map/place_pieces/pallas_call | solution.py:316
  143.1 2.8 %collective-permute-start.21 = (bf16[256,640]{1,0:T(8,128)(2,1)}, bf16[256,640]{1,0:T(8,128)(2,1)}, u32[]{:S(2)}, u32[]{:S(2)}) collective-permute-start(bf16[256,640]{1,0:T(8,128)(2,1)} %fusion), channel_id=1, source_target_pairs={{0,1},{1,0},{2,3},{3,2},{4,5},{5,4},{6,7},{7,6},{8,9},{9,8},{10,11... | collective-permute-start | bytes 983048 | tf_op jit(solution)/shard_map/ppermute | solution.py:31
  147.3 4.4 %place_pieces.5.refs_5_ = bf16[1024,16,256]{2,1,0:T(8,128)(2,1)} custom-call(s32[8]{0:T(128)} %stack.62.places_ref, bf16[128,16,256]{2,1,0:T(8,128)(2,1)} %get-tuple-element.61.refs_0_, bf16[128,16,256]{2,1,0:T(8,128)(2,1)} %copy-done.1, bf16[128,16,256]{2,1,0:T(8,128)(2,1)} %copy-done, bf16[128,16,256]{2,1,0:T(8,128)(2,1)} %copy-done.2, ...), custom_call_target="tpu_custom_call" | custom-call | bytes 16777216 | tf_op jit(solution)/shard_map/place_pieces/pallas_call | solution.py:316
  157.3 4.2 %place_pieces.7 = bf16[1024,16,256]{2,1,0:T(8,128)(2,1)} custom-call(s32[8]{0:T(128)} %stack.71.places_ref, bf16[128,16,256]{2,1,0:T(8,128)(2,1)} %get-tuple-element.72.refs_0_, bf16[128,16,256]{2,1,0:T(8,128)(2,1)} %copy-done.4, bf16[128,16,256]{2,1,0:T(8,128)(2,1)} %copy-done.3, bf16[128,16,256]{2,1,0:T(8,128)(2,1)} %copy-done.5, ...), custom_call_target="tpu_custom_call", output_to_operand_aliasing={{}: (6, {})} | custom-call | bytes 16777216 | tf_op jit(solution)/shard_map/place_pieces/pallas_call | solution.py:316
  (105 shorter events, 36.0 us)
Async XLA Ops:
  0.6 19.6 %collective-permute-start = (bf16[4,128,640]{2,1,0:T(8,128)(2,1)}, bf16[4,128,640]{2,1,0:T(8,128)(2,1)S(1)}, u32[]{:S(2)}, u32[]{:S(2)}) collective-permute-start(bf16[4,128,640]{2,1,0:T(8,128)(2,1)} %x0.2), channel_id=1, source_target_pairs={{0,1},{1,0},{2,3},{3,2},{4,5},{5,4},{6,7},{7,6},{8,9},{9,8},{10,11... | collective-permute-start | bytes 1966088 | tf_op jit(solution)/shard_map/ppermute | solution.py:31
  5.1 20.6 %collective-permute-start.3 = (bf16[4,128,640]{2,1,0:T(8,128)(2,1)}, bf16[4,128,640]{2,1,0:T(8,128)(2,1)S(1)}, u32[]{:S(2)}, u32[]{:S(2)}) collective-permute-start(bf16[4,128,640]{2,1,0:T(8,128)(2,1)} %x0.2), channel_id=1, source_target_pairs={{0,2},{1,3},{2,4},{3,5},{4,6},{5,7},{6,0},{7,1},{8,10},{9,11},{10,... | collective-permute-start | bytes 1966088 | tf_op jit(solution)/shard_map/ppermute | solution.py:31
  6.4 19.3 %collective-permute-start.2 = (bf16[4,128,640]{2,1,0:T(8,128)(2,1)}, bf16[4,128,640]{2,1,0:T(8,128)(2,1)S(1)}, u32[]{:S(2)}, u32[]{:S(2)}) collective-permute-start(bf16[4,128,640]{2,1,0:T(8,128)(2,1)} %x0.2), channel_id=1, source_target_pairs={{0,6},{1,7},{2,0},{3,1},{4,2},{5,3},{6,4},{7,5},{8,14},{9,15},{10,... | collective-permute-start | bytes 1966088 | tf_op jit(solution)/shard_map/ppermute | solution.py:31
  20.2 15.7 %collective-permute-start.5 = (bf16[4,128,640]{2,1,0:T(8,128)(2,1)S(1)}, bf16[4,128,640]{2,1,0:T(8,128)(2,1)S(1)}, u32[]{:S(2)}, u32[]{:S(2)}) collective-permute-start(bf16[4,128,640]{2,1,0:T(8,128)(2,1)S(1)} %collective-permute-done.x1), channel_id=1, source_target_pairs={{0,6},{1,7},{2,0},{3,1},{4,2},{5,3},{6,4},{7,5},{8,14},{9,15},{10,... | collective-permute-start | bytes 1966088 | tf_op jit(solution)/shard_map/ppermute | solution.py:31
  23.0 24.5 %collective-permute-start.13 = (bf16[128,16,256]{2,1,0:T(8,128)(2,1)}, bf16[128,16,256]{2,1,0:T(8,128)(2,1)S(1)}, u32[]{:S(2)}, u32[]{:S(2)}) collective-permute-start(bf16[128,16,256]{2,1,0:T(8,128)(2,1)} %get-tuple-element.47), channel_id=1, source_target_pairs={{0,32},{8,40},{16,48},{24,56},{32,0},{40,8},{48,16},{56,24},{64,96... | collective-permute-start | bytes 3145736 | tf_op jit(solution)/shard_map/ppermute | solution.py:41
  25.7 52.8 %collective-permute-start.16 = (bf16[256,16,256]{2,1,0:T(8,128)(2,1)}, bf16[256,16,256]{2,1,0:T(8,128)(2,1)}, u32[]{:S(2)}, u32[]{:S(2)}) collective-permute-start(bf16[256,16,256]{2,1,0:T(8,128)(2,1)} %get-tuple-element.44), channel_id=1, source_target_pairs={{0,64},{8,72},{16,80},{24,88},{32,96},{40,104},{48,112},{56,120},{... | collective-permute-start | bytes 6291464 | tf_op jit(solution)/shard_map/ppermute | solution.py:41
  26.5 29.1 %collective-permute-start.6 = (bf16[4,128,640]{2,1,0:T(8,128)(2,1)S(1)}, bf16[4,128,640]{2,1,0:T(8,128)(2,1)S(1)}, u32[]{:S(2)}, u32[]{:S(2)}) collective-permute-start(bf16[4,128,640]{2,1,0:T(8,128)(2,1)S(1)} %collective-permute-done.x1), channel_id=1, source_target_pairs={{0,2},{1,3},{2,4},{3,5},{4,6},{5,7},{6,0},{7,1},{8,10},{9,11},{10,... | collective-permute-start | bytes 1966088 | tf_op jit(solution)/shard_map/ppermute | solution.py:31
  26.6 29.1 %collective-permute-start.4 = (bf16[4,128,640]{2,1,0:T(8,128)(2,1)S(1)}, bf16[4,128,640]{2,1,0:T(8,128)(2,1)S(1)}, u32[]{:S(2)}, u32[]{:S(2)}) collective-permute-start(bf16[4,128,640]{2,1,0:T(8,128)(2,1)S(1)} %collective-permute-done.3.x3), channel_id=1, source_target_pairs={{0,2},{1,3},{2,4},{3,5},{4,6},{5,7},{6,0},{7,1},{8,10},{9,11},{10,... | collective-permute-start | bytes 1966088 | tf_op jit(solution)/shard_map/ppermute | solution.py:31
  35.9 19.7 %collective-permute-start.7 = (bf16[4,128,640]{2,1,0:T(8,128)(2,1)S(1)}, bf16[4,128,640]{2,1,0:T(8,128)(2,1)S(1)}, u32[]{:S(2)}, u32[]{:S(2)}) collective-permute-start(bf16[4,128,640]{2,1,0:T(8,128)(2,1)S(1)} %collective-permute-done.5.x5), channel_id=1, source_target_pairs={{0,6},{1,7},{2,0},{3,1},{4,2},{5,3},{6,4},{7,5},{8,14},{9,15},{10,... | collective-permute-start | bytes 1966088 | tf_op jit(solution)/shard_map/ppermute | solution.py:31
  55.7 22.8 %collective-permute-start.14 = (bf16[128,16,256]{2,1,0:T(8,128)(2,1)}, bf16[128,16,256]{2,1,0:T(8,128)(2,1)S(1)}, u32[]{:S(2)}, u32[]{:S(2)}) collective-permute-start(bf16[128,16,256]{2,1,0:T(8,128)(2,1)} %get-tuple-element.48), channel_id=1, source_target_pairs={{0,16},{8,24},{16,32},{24,40},{32,48},{40,56},{48,0},{56,8},{64,80... | collective-permute-start | bytes 3145736 | tf_op jit(solution)/shard_map/ppermute | solution.py:41
  56.9 21.6 %collective-permute-start.15 = (bf16[128,16,256]{2,1,0:T(8,128)(2,1)}, bf16[128,16,256]{2,1,0:T(8,128)(2,1)S(1)}, u32[]{:S(2)}, u32[]{:S(2)}) collective-permute-start(bf16[128,16,256]{2,1,0:T(8,128)(2,1)} %get-tuple-element.50), channel_id=1, source_target_pairs={{0,48},{8,56},{16,0},{24,8},{32,16},{40,24},{48,32},{56,40},{64,11... | collective-permute-start | bytes 3145736 | tf_op jit(solution)/shard_map/ppermute | solution.py:41
  74.5 12.7 %collective-permute-start.8 = (bf16[2,256,640]{2,1,0:T(8,128)(2,1)}, bf16[2,256,640]{2,1,0:T(8,128)(2,1)}, u32[]{:S(2)}, u32[]{:S(2)}) collective-permute-start(bf16[2,256,640]{2,1,0:T(8,128)(2,1)} %get-tuple-element.42), channel_id=1, source_target_pairs={{0,6},{1,7},{2,0},{3,1},{4,2},{5,3},{6,4},{7,5},{8,14},{9,15},{10,... | collective-permute-start | bytes 1966088 | tf_op jit(solution)/shard_map/ppermute | solution.py:31
  74.6 14.1 %collective-permute-start.9 = (bf16[2,256,640]{2,1,0:T(8,128)(2,1)}, bf16[2,256,640]{2,1,0:T(8,128)(2,1)}, u32[]{:S(2)}, u32[]{:S(2)}) collective-permute-start(bf16[2,256,640]{2,1,0:T(8,128)(2,1)} %get-tuple-element.43), channel_id=1, source_target_pairs={{0,2},{1,3},{2,4},{3,5},{4,6},{5,7},{6,0},{7,1},{8,10},{9,11},{10,... | collective-permute-start | bytes 1966088 | tf_op jit(solution)/shard_map/ppermute | solution.py:31
  83.1 27.4 %collective-permute-start.23 = (bf16[128,16,256]{2,1,0:T(8,128)(2,1)}, bf16[128,16,256]{2,1,0:T(8,128)(2,1)S(1)}, u32[]{:S(2)}, u32[]{:S(2)}) collective-permute-start(bf16[128,16,256]{2,1,0:T(8,128)(2,1)} %get-tuple-element.68), channel_id=1, source_target_pairs={{0,32},{8,40},{16,48},{24,56},{32,0},{40,8},{48,16},{56,24},{64,96... | collective-permute-start | bytes 3145736 | tf_op jit(solution)/shard_map/ppermute | solution.py:41
  90.9 16.8 %collective-permute-start.11 = (bf16[256,640]{1,0:T(8,128)(2,1)}, bf16[256,640]{1,0:T(8,128)(2,1)S(1)}, u32[]{:S(2)}, u32[]{:S(2)}) collective-permute-start(bf16[256,640]{1,0:T(8,128)(2,1)} %get-tuple-element.78), channel_id=1, source_target_pairs={{0,6},{1,7},{2,0},{3,1},{4,2},{5,3},{6,4},{7,5},{8,14},{9,15},{10,... | collective-permute-start | bytes 983048 | tf_op jit(solution)/shard_map/ppermute | solution.py:31
  91.0 16.8 %collective-permute-start.10 = (bf16[256,640]{1,0:T(8,128)(2,1)S(1)}, bf16[256,640]{1,0:T(8,128)(2,1)S(1)}, u32[]{:S(2)}, u32[]{:S(2)}) collective-permute-start(bf16[256,640]{1,0:T(8,128)(2,1)S(1)} %get-tuple-element.79), channel_id=1, source_target_pairs={{0,2},{1,3},{2,4},{3,5},{4,6},{5,7},{6,0},{7,1},{8,10},{9,11},{10,... | collective-permute-start | bytes 983048 | tf_op jit(solution)/shard_map/ppermute | solution.py:31
  107.8 12.4 %collective-permute-start.18 = (bf16[2,256,640]{2,1,0:T(8,128)(2,1)}, bf16[2,256,640]{2,1,0:T(8,128)(2,1)S(1)}, u32[]{:S(2)}, u32[]{:S(2)}) collective-permute-start(bf16[2,256,640]{2,1,0:T(8,128)(2,1)} %get-tuple-element.58), channel_id=1, source_target_pairs={{0,2},{1,3},{2,4},{3,5},{4,6},{5,7},{6,0},{7,1},{8,10},{9,11},{10,... | collective-permute-start | bytes 1966088 | tf_op jit(solution)/shard_map/ppermute | solution.py:31
  110.6 28.0 %collective-permute-start.24 = (bf16[128,16,256]{2,1,0:T(8,128)(2,1)}, bf16[128,16,256]{2,1,0:T(8,128)(2,1)S(1)}, u32[]{:S(2)}, u32[]{:S(2)}) collective-permute-start(bf16[128,16,256]{2,1,0:T(8,128)(2,1)} %get-tuple-element.69), channel_id=1, source_target_pairs={{0,16},{8,24},{16,32},{24,40},{32,48},{40,56},{48,0},{56,8},{64,80... | collective-permute-start | bytes 3145736 | tf_op jit(solution)/shard_map/ppermute | solution.py:41
  110.7 27.8 %collective-permute-start.25 = (bf16[128,16,256]{2,1,0:T(8,128)(2,1)}, bf16[128,16,256]{2,1,0:T(8,128)(2,1)S(1)}, u32[]{:S(2)}, u32[]{:S(2)}) collective-permute-start(bf16[128,16,256]{2,1,0:T(8,128)(2,1)} %get-tuple-element.71), channel_id=1, source_target_pairs={{0,48},{8,56},{16,0},{24,8},{32,16},{40,24},{48,32},{56,40},{64,11... | collective-permute-start | bytes 3145736 | tf_op jit(solution)/shard_map/ppermute | solution.py:41
  114.5 13.3 %collective-permute-start.12 = (bf16[256,640]{1,0:T(8,128)(2,1)S(1)}, bf16[256,640]{1,0:T(8,128)(2,1)}, u32[]{:S(2)}, u32[]{:S(2)}) collective-permute-start(bf16[256,640]{1,0:T(8,128)(2,1)S(1)} %fusion.3), channel_id=1, source_target_pairs={{0,1},{1,0},{2,3},{3,2},{4,5},{5,4},{6,7},{7,6},{8,9},{9,8},{10,11... | collective-permute-start | bytes 983048 | tf_op jit(solution)/shard_map/ppermute | solution.py:31
  121.4 15.2 %collective-permute-start.19 = (bf16[256,640]{1,0:T(8,128)(2,1)}, bf16[256,640]{1,0:T(8,128)(2,1)S(1)}, u32[]{:S(2)}, u32[]{:S(2)}) collective-permute-start(bf16[256,640]{1,0:T(8,128)(2,1)} %get-tuple-element.76), channel_id=1, source_target_pairs={{0,2},{1,3},{2,4},{3,5},{4,6},{5,7},{6,0},{7,1},{8,10},{9,11},{10,... | collective-permute-start | bytes 983048 | tf_op jit(solution)/shard_map/ppermute | solution.py:31
  121.5 15.1 %collective-permute-start.20 = (bf16[256,640]{1,0:T(8,128)(2,1)}, bf16[256,640]{1,0:T(8,128)(2,1)S(1)}, u32[]{:S(2)}, u32[]{:S(2)}) collective-permute-start(bf16[256,640]{1,0:T(8,128)(2,1)} %get-tuple-element.77), channel_id=1, source_target_pairs={{0,6},{1,7},{2,0},{3,1},{4,2},{5,3},{6,4},{7,5},{8,14},{9,15},{10,... | collective-permute-start | bytes 983048 | tf_op jit(solution)/shard_map/ppermute | solution.py:31
  127.8 19.5 %collective-permute-start.22 = (bf16[256,16,256]{2,1,0:T(8,128)(2,1)}, bf16[256,16,256]{2,1,0:T(8,128)(2,1)}, u32[]{:S(2)}, u32[]{:S(2)}) collective-permute-start(bf16[256,16,256]{2,1,0:T(8,128)(2,1)} %place_pieces.4), channel_id=1, source_target_pairs={{0,8},{8,0},{16,24},{24,16},{32,40},{40,32},{48,56},{56,48},{64,72... | collective-permute-start | bytes 6291464 | tf_op jit(solution)/shard_map/ppermute | solution.py:41
  143.0 13.0 %collective-permute-start.26 = (bf16[256,16,256]{2,1,0:T(8,128)(2,1)}, bf16[256,16,256]{2,1,0:T(8,128)(2,1)S(1)}, u32[]{:S(2)}, u32[]{:S(2)}) collective-permute-start(bf16[256,16,256]{2,1,0:T(8,128)(2,1)} %place_pieces.6), channel_id=1, source_target_pairs={{0,8},{8,0},{16,24},{24,16},{32,40},{40,32},{48,56},{56,48},{64,72... | collective-permute-start | bytes 6291464 | tf_op jit(solution)/shard_map/ppermute | solution.py:41
  (27 other events, 319.9 us)
